TPU v7x, 128 devices: a whole 4x4x4 slice. The times are simulated.
128 devices in a mesh: gx: 16 (over x, y), gy: 8 (over z, core).
Axes of the slice: x: 4, y: 4, z: 4, core: 2. Of those that a mesh axis runs over, the one named last changes fastest.
Arguments:
- dynamics: float32 [3, 72, 8192], P(None, None, ('gx', 'gy')), may hold values from -6 to 6
- crm_state: float32 [4, 58, 64, 8192], P(None, None, None, ('gx', 'gy')), may hold values from -6 to 6
- density: float32 [58], replicated, may hold values from 0.3 to 1.5
- orientation: int32 [8192], P(('gx', 'gy')), may hold values from 0 to 1
- owner: int32 [8192], P(('gx', 'gy')), may hold values from 0 to 15, as said below
- active: int32 [8192], P(('gx', 'gy')), may hold values from 14 to 58
Outputs:
- dynamics_next: float32 [3, 72, 8192], P(None, None, ('gx', 'gy'))
- crm_next: float32 [4, 58, 64, 16384], P(None, None, None, ('gx', 'gy'))
Inputs may be any that keep to these rules, and one draw needn't show every extreme that they name: Among one device's columns at most 8 have any one owner; for every gy index some owner receives exactly 8 columns from every device with that gy index. `orientation`: 0 for the first horizontal direction, 1 for the second.
All inputs are finite; a program needn't handle non-finite values.
Results may differ from a plain program's by a relative error of at most 0.0003.
Values sent between devices are 32-bit elements; how exact they have to be, the bound alone decides.
No kernel may reach another device: no remote copies, remote signals or barrier semaphores. Data moves between devices by JAX's collectives and lax.ppermute only.
A program may use at most 128 MiB of HBM per device.

v0:
```python
import jax
import jax.numpy as jnp
from jax import lax
from jax.sharding import PartitionSpec as P

NSTEP = 2
ITERS = 8
TX = 8
TY = 8


def extended(cells, sides, width):
    for axis, dim in sides:
        count = lax.axis_size(axis)
        head = lax.slice_in_dim(cells, 0, width, axis=dim)
        tail = lax.slice_in_dim(cells, cells.shape[dim] - width, cells.shape[dim], axis=dim)
        cells = jnp.concatenate(
            [
                lax.ppermute(tail, axis, [(i, (i + 1) % count) for i in range(count)]),
                cells,
                lax.ppermute(head, axis, [((i + 1) % count, i) for i in range(count)]),
            ],
            axis=dim,
        )
    return cells


def shift_up(field):
    return jnp.concatenate([field[1:], jnp.zeros_like(field[:1])], axis=0)


def shift_down(field):
    return jnp.concatenate([jnp.zeros_like(field[:1]), field[:-1]], axis=0)


def lap_x(field):
    return jnp.roll(field, 1, axis=1) + jnp.roll(field, -1, axis=1) - 2.0 * field


def cloud_model(state, force_b, force_u, active_f, density):
    nz = state.shape[1]
    levels = jnp.arange(nz, dtype=jnp.float32)[:, None, None]
    mask = (levels < active_f).astype(jnp.float32)
    rho = density[:, None, None]
    rho_up = 0.5 * (rho + shift_up(rho)) * (levels < nz - 1).astype(jnp.float32)
    rho_dn = shift_down(rho_up)
    diag_term = -(2.0 * rho + rho_up + rho_dn + 0.1 * rho)
    u_wind, w_wind, buoy, press = (state[0], state[1], state[2], state[3])
    u_start, b_start = (u_wind, buoy)

    def sweep(step, press):
        applied = (
            rho * lap_x(press)
            + rho_up * (shift_up(press) - press)
            - rho_dn * (press - shift_down(press))
            - 0.1 * rho * press
        )
        return press + 0.8 * (rhs_now - applied) / diag_term

    for step in range(NSTEP):
        mean_b = jnp.mean(buoy, axis=1, keepdims=True)
        mean_u = jnp.mean(u_wind, axis=1, keepdims=True)
        b_next = buoy + 0.25 * (force_b - mean_b) + 0.2 * lap_x(buoy) - 0.5 * w_wind
        u_next = u_wind + 0.25 * (force_u - mean_u) + 0.2 * lap_x(u_wind)
        w_next = w_wind + buoy
        flux = rho * w_next
        rhs_now = 0.5 * rho * (jnp.roll(u_next, -1, axis=1) - jnp.roll(u_next, 1, axis=1)) + 0.5 * (
            shift_up(flux) - shift_down(flux)
        )
        press = lax.fori_loop(0, ITERS, sweep, press)
        u_wind = mask * (u_next - 0.5 * (jnp.roll(press, -1, axis=1) - jnp.roll(press, 1, axis=1)))
        w_wind = mask * (w_next - 0.5 * (shift_up(press) - shift_down(press)))
        buoy = mask * b_next
    tend_b = jnp.mean(buoy - b_start, axis=1, keepdims=True) / NSTEP
    tend_u = jnp.mean(u_wind - u_start, axis=1, keepdims=True) / NSTEP
    return (jnp.stack([u_wind, w_wind, buoy, press]), jnp.stack([tend_b, tend_u]))


def place_rows(field, table):
    lead = field.shape[:-1]
    flat = field.reshape(-1, field.shape[-1])
    placed = jnp.dot(
        flat, table, preferred_element_type=jnp.float32, precision=lax.Precision.HIGHEST
    )
    return placed.reshape(lead + (table.shape[1],))


def per_device(dynamics, crm_state, density, orientation, owner, active):
    groups = lax.axis_size("gx")
    cols = owner.shape[0]
    nzc = crm_state.shape[1]
    levels = dynamics.shape[1]
    cap = 2 * cols // groups
    onehot = (owner[:, None] == jnp.arange(groups, dtype=jnp.int32)[None, :]).astype(jnp.int32)
    rank = jnp.sum(jnp.cumsum(onehot, axis=0) * onehot, axis=1) - 1
    slot = owner * cap + rank
    match = (slot[:, None] == jnp.arange(2 * cols, dtype=jnp.int32)[None, :]).astype(jnp.float32)
    force_b = dynamics[0, :nzc]
    force_u = jnp.where(orientation[None, :] == 0, dynamics[1, :nzc], dynamics[2, :nzc])
    active_f = active.astype(jnp.float32)[None, :]
    sent_state = place_rows(crm_state, match)
    sent_force = jnp.stack([place_rows(force_b, match), place_rows(force_u, match)])[:, :, None, :]
    sent_active = place_rows(active_f, match)[None, None]
    got_state, got_force, got_active = (
        lax.all_to_all(sent_state, "gx", split_axis=3, concat_axis=3, tiled=True),
        lax.all_to_all(sent_force, "gx", split_axis=3, concat_axis=3, tiled=True),
        lax.all_to_all(sent_active, "gx", split_axis=3, concat_axis=3, tiled=True),
    )
    crm_next, owner_tends = cloud_model(
        got_state, got_force[0], got_force[1], got_active[0], density
    )
    returned = lax.all_to_all(owner_tends, "gx", split_axis=3, concat_axis=3, tiled=True)
    tends = place_rows(returned[:, :, 0, :], match.T)
    pad = jnp.zeros((levels - nzc, cols), jnp.float32)
    add_b = jnp.concatenate([tends[0], pad], axis=0)
    add_u = jnp.concatenate([tends[1], pad], axis=0)
    first = (orientation[None, :] == 0).astype(jnp.float32)
    adds = jnp.stack([add_b, first * add_u, (1.0 - first) * add_u])
    grid = dynamics.reshape(3, levels, TX, TY)
    padded = extended(grid, (("gx", 2), ("gy", 3)), 1)
    laplace = (
        padded[:, :, 2:, 1:-1]
        + padded[:, :, :-2, 1:-1]
        + padded[:, :, 1:-1, 2:]
        + padded[:, :, 1:-1, :-2]
        - 4.0 * grid
    )
    dynamics_next = (grid + 0.2 * laplace).reshape(3, levels, cols) + adds
    return (dynamics_next, crm_next)


def solution(mesh):
    in_specs = (
        P(None, None, ("gx", "gy")),
        P(None, None, None, ("gx", "gy")),
        P(),
        P(("gx", "gy")),
        P(("gx", "gy")),
        P(("gx", "gy")),
    )
    out_specs = (P(None, None, ("gx", "gy")), P(None, None, None, ("gx", "gy")))
    return jax.shard_map(
        per_device, mesh=mesh, in_specs=in_specs, out_specs=out_specs, check_vma=False
    )
```

profile of v0, /device:TPU:0, one launch (start us, length us, event | category | flops | bytes accessed | tf_op | source)
XLA Modules:
  0.0 551.0 jit_solution(10231098971782247088)
XLA Ops:
  3.0 1.6 fusion.76
  4.6 7.1 %all-to-all-start = ((f32[1,1,1,128]{2,1,0,3:T(1,128)}), f32[1,1,1,128]{2,1,0,3:T(1,128)S(1)}, u32[]{:S(2)}, u32[]{:S(2)}) async-start(f32[1,1,1,128]{2,1,0,3:T(1,128)} %bitcast.75), calls=%async_computation | async-start | bytes 131072 | tf_op jit(solution)/shard_map/all_to_all | solution.py:107
  16.0 3.3 all-to-all-done
  19.4 3.9 all-to-all-start.2
  23.3 10.8 %convolution_bitcast_fusion = f32[14848,128]{0,1:T(8,128)} fusion(f32[14848,64]{1,0:T(8,128)} %bitcast.188, s32[64]{0:T(128)S(1)} %add_add_fusion), kind=kOutput, calls=%fused_computation.22 | convolution fusion | flops 1459634176 | bytes 11403520 | tf_op jit(solution)/shard_map/dot_general | solution.py:82
  34.1 8.7 %copy.245 = f32[14848,128]{1,0:T(8,128)} copy(f32[14848,128]{0,1:T(8,128)} %convolution_bitcast_fusion) | data formatting | bytes 15204352 | tf_op jit(solution)/shard_map/dot_general | solution.py:82
  42.8 15.2 %copy.246 = f32[4,58,64,128]{2,0,1,3:T(4,128)} copy(f32[4,58,64,128]{3,2,1,0:T(8,128)} %bitcast.187) | data formatting | bytes 15204352 | tf_op jit(solution)/shard_map/reshape | solution.py:85
  58.0 20.0 %reshape.401 = f32[16,1,118784]{2,1,0:T(1,128)} reshape(f32[128,58,4,64]{3,2,1,0:T(4,128)} %bitcast.186) | data formatting | bytes 15204352
  78.0 7.4 %all-to-all-start.1 = ((f32[16,1,118784]{2,1,0:T(1,128)}), f32[16,1,118784]{2,1,0:T(1,128)}, u32[]{:S(2)}, u32[]{:S(2)}) async-start(f32[16,1,118784]{2,1,0:T(1,128)} %reshape.401), calls=%async_computation.1 | async-start | bytes 15204352 | tf_op jit(solution)/shard_map/all_to_all | solution.py:105
  85.5 5.3 collective-permute-start
  92.9 86.5 %collective-permute-done = f32[3,72,1,8]{1,3,2,0:T(8,128)S(1)} collective-permute-done((f32[3,72,1,8]{1,3,2,0:T(8,128)S(1)}, f32[3,72,1,8]{1,3,2,0:T(8,128)S(1)}, u32[]{:S(2)}, u32[]{:S(2)}) %collective-permute-start) | collective-permute-done | bytes 6944 | tf_op jit(solution)/shard_map/ppermute | solution.py:21
  180.0 3.0 collective-permute-start.2
  184.9 19.9 %all-to-all-done.1 = f32[16,1,118784]{2,1,0:T(1,128)} async-done(((f32[16,1,118784]{2,1,0:T(1,128)}), f32[16,1,118784]{2,1,0:T(1,128)}, u32[]{:S(2)}, u32[]{:S(2)}) %all-to-all-start.1) | async-done | bytes 7602208 | tf_op jit(solution)/shard_map/all_to_all | solution.py:105
  204.8 44.0 %reduce.3 = f32[16,118784]{1,0:T(8,128)} reduce(f32[16,1,118784]{2,1,0:T(1,128)} %all-to-all-done.1, f32[]{:T(128)} %broadcast.295), dimensions={1}, to_apply=%all_to_all.13.reduce_sub_computation | reduce | bytes 15204356 | tf_op jit(solution)/shard_map/all_to_all | solution.py:105
  248.8 20.6 %reshape.402 = f32[128,58,4,64]{3,2,1,0:T(4,128)} reshape(f32[16,118784]{1,0:T(8,128)} %reduce.3) | data formatting | bytes 15204352
  269.4 73.7 %slice_reduce_fusion.1 = (f32[58,128]{0,1:T(8,128)S(1)}, f32[58,128]{0,1:T(8,128)S(1)}, f32[1,58,64,128]{2,0,1,3:T(1,128)}, f32[1,58,64,128]{2,0,1,3:T(1,128)}, ...) fusion(f32[4,58,64,128]{2,0,1,3:T(4,128)} %bitcast.185), kind=kLoop, calls=%fused_computation.169 | loop fusion | flops 935424 | bytes 15263744 | tf_op jit(solution)/shard_map/reduce_sum | solution.py:61
  343.1 7.4 %copy.269 = f32[1,58,64,128]{3,2,1,0:T(8,128)S(1)} copy(f32[1,58,64,128]{2,0,1,3:T(1,128)} %get-tuple-element.176) | data formatting | bytes 3801088
  350.5 3.6 slice_bitcast_fusion.12
  354.3 2.7 fusion.30
  357.0 2.5 fusion.109
  359.5 7.4 %copy.265 = f32[1,58,64,128]{3,2,1,0:T(8,128)S(1)} copy(f32[1,58,64,128]{2,0,1,3:T(1,128)} %get-tuple-element.173) | data formatting | bytes 3801088
  367.0 2.5 fusion.104
  369.5 7.4 %copy.268 = f32[1,58,64,128]{3,2,1,0:T(8,128)S(1)} copy(f32[1,58,64,128]{2,0,1,3:T(1,128)} %get-tuple-element.175) | data formatting | bytes 3801088
  376.9 8.5 %copy.267 = f32[1,58,64,128]{3,2,1,0:T(8,128)} copy(f32[1,58,64,128]{2,0,1,3:T(1,128)} %get-tuple-element.174) | data formatting | bytes 3801088
  385.5 2.3 broadcast_multiply_fusion.2
  389.9 1.9 fusion.32
  391.7 30.4 %while.20 = (s32[]{:T(128)}, f32[58,64,128]{2,1,0:T(8,128)S(1)}, f32[58,1,1]{0,2,1:T(1,128)S(1)}, f32[58,1,1]{0,2,1:T(1,128)S(1)}, f32[58,1,1]{0,2,1:T(1,128)S(1...) while((s32[]{:T(128)}, f32[58,64,128]{2,1,0:T(8,128)S(1)}, f32[58,1,1]{0,2,1:T(1,128)S(1)}, ...), condition=%wide.region_6.7_spmd, body=%wide.region_5.6_spmd.sunk | while | flops 8552508 | bytes 35915464 | solution.py:70
  393.8 1.8 fusion.126
  397.6 1.8 fusion.126
  401.4 1.8 fusion.126
  405.2 1.8 fusion.126
  409.0 1.8 fusion.126
  412.8 1.8 fusion.126
  416.6 1.8 fusion.126
  420.4 1.8 fusion.126
  423.4 60.0 %while.21 = (s32[]{:T(128)}, f32[58,64,128]{2,1,0:T(8,128)}, f32[58,1,1]{0,2,1:T(1,128)S(1)}, f32[58,1,1]{0,2,1:T(1,128)S(1)}, f32[58,1,1]{0,2,1:T(1,128)S(1)}, ...) while((s32[]{:T(128)}, f32[58,64,128]{2,1,0:T(8,128)}, f32[58,1,1]{0,2,1:T(1,128)S(1)}, ...), condition=%wide.region_10.11_spmd, body=%wide.region_9.10_spmd.sunk | while | flops 8552508 | bytes 51119872 | solution.py:70
  423.7 2.9 fusion.127
  428.2 1.7 fusion.130
  431.2 2.9 fusion.127
  435.6 1.7 fusion.130
  438.6 2.9 fusion.127
  443.1 1.7 fusion.130
  446.1 2.9 fusion.127
  450.6 1.7 fusion.130
  453.6 2.9 fusion.127
  458.0 1.7 fusion.130
  461.0 2.9 fusion.127
  465.5 1.7 fusion.130
  468.5 2.9 fusion.127
  473.0 1.7 fusion.130
  476.0 2.9 fusion.127
  480.4 1.7 fusion.130
  483.4 5.4 fusion.105
  489.0 8.1 %multiply_bitcast_fusion = (f32[1,58,64,128]{3,2,1,0:T(8,128)}, f32[58,64,128]{2,1,0:T(8,128)}, f32[58,64,128]{2,1,0:T(8,128)S(1)}) fusion(f32[57,64,128]{2,1,0:T(8,128)} %get-tuple-element.243, f32[57,64,128]{2,1,0:T(8,128)} %get-tuple-element.244, f32[58,128]{1,0:T(8,128)S(1)} %fusion.78, f32[57,64,128]{2,1,0:T(8,128)} %get-tuple-element.218, ...), kind=kLoop, calls=%fused_computation.75 | loop fusion | flops 9977856 | bytes 20834304 | tf_op jit(solution)/shard_map/stack | solution.py:76
  497.1 2.2 fusion.102
  500.0 6.1 %slice_bitcast_fusion.13 = (f32[1,58,63,128]{3,2,1,0:T(8,128)}, f32[1,58,63,128]{3,2,1,0:T(8,128)}, f32[58,63,128]{2,1,0:T(8,128)}, f32[58,63,128]{2,1,0:T(8,128...) fusion(f32[58,64,128]{2,1,0:T(8,128)S(1)} %copy-done.2, ...), kind=kLoop, calls=%fused_computation.164 | loop fusion | bytes 22450176 | tf_op jit(solution)/shard_map/jit(_roll_static)/concatenate | solution.py:71
  506.3 1.9 reduce_sum.65
  508.4 6.8 %subtract_reduce_fusion = (f32[58,128]{1,0:T(8,128)S(1)}, f32[58,64,128]{2,1,0:T(8,128)}, f32[58,128]{1,0:T(8,128)S(1)}, f32[58,64,128]{2,1,0:T(8,128)S(1)}) fusion(f32[1,58,64,128]{3,2,1,0:T(8,128)S(1)} %copy-done.9, f32[58,64,128]{2,1,0:T(8,128)} %get-tuple-element.155, f32[58,64,128]{2,1,0:T(8,128)} %copy-done.10, ...), kind=kLoop, calls=%fused_computation.76 | loop fusion | flops 9487872 | bytes 19124224 | tf_op jit(solution)/shard_map/reduce_sum | solution.py:74
  515.2 2.4 slice_bitcast_fusion.9
  519.2 2.0 fusion.42
  522.3 14.4 %all-to-all-start.3 = ((f32[16,1,928]{2,1,0:T(1,128)}), f32[16,1,928]{2,1,0:T(1,128)S(1)}, u32[]{:S(2)}, u32[]{:S(2)}) async-start(f32[16,1,928]{2,1,0:T(1,128)} %reshape.405), calls=%async_computation.3 | async-start | bytes 131072 | tf_op jit(solution)/shard_map/all_to_all | solution.py:112
  536.7 6.8 %fusion.54 = f32[1,58,64,128]{3,2,1,0:T(8,128)S(1)} fusion(f32[1,58,63,128]{3,2,1,0:T(8,128)} %get-tuple-element.204, f32[1,58,1,128]{3,2,1,0:T(1,128)S(1)} %get-tuple-element.206, f32[1,58,1,128]{3,2,1,0:T(1,128)S(1)} %get-tuple-element.205, f32[1,58,63,128]{3,2,1,0:T(8,128)} %get-tuple-element.201, f32[1,58,1,128]{3,2,1,0:T(1,128)S(1)} %get-tuple-element.194, ...), kind=kLoop, calls=%fused_computation.70 | loop fusion | flops 13303808 | bytes 19094528 | tf_op jit(solution)/shard_map/mul | solution.py:71
  543.8 3.6 pad_maximum_fusion
  549.1 1.5 fusion.61
  (233 shorter events, 58.7 us)
Async XLA Ops:
  3.0 31.1 %copy-start.25 = (s32[64]{0:T(128)}, s32[64]{0:T(128)S(1)}, u32[]{:S(2)}) copy-start(s32[64]{0:T(128)S(1)} %add_add_fusion) | copy-start | bytes 772
  4.6 14.8 %all-to-all-start = ((f32[1,1,1,128]{2,1,0,3:T(1,128)}), f32[1,1,1,128]{2,1,0,3:T(1,128)S(1)}, u32[]{:S(2)}, u32[]{:S(2)}) async-start(f32[1,1,1,128]{2,1,0,3:T(1,128)} %bitcast.75), calls=%async_computation | async-start | bytes 131072 | tf_op jit(solution)/shard_map/all_to_all | solution.py:107
  19.4 58.7 %all-to-all-start.2 = ((f32[16,1,928]{2,1,0:T(1,128)}), f32[16,1,928]{2,1,0:T(1,128)S(1)}, u32[]{:S(2)}, u32[]{:S(2)}) async-start(f32[16,1,928]{2,1,0:T(1,128)} %reshape.403), calls=%async_computation.2 | async-start | bytes 131072 | tf_op jit(solution)/shard_map/all_to_all | solution.py:106
  78.0 7.4 %copy-start.18 = (f32[3,72,64]{1,2,0:T(8,128)S(1)}, f32[3,72,64]{1,2,0:T(8,128)}, u32[]{:S(2)}) copy-start(f32[3,72,64]{1,2,0:T(8,128)} %param.10) | copy-start | bytes 165892
  78.0 12.9 %copy-start.20 = (f32[58]{0:T(128)S(1)}, f32[58]{0:T(128)}, u32[]{:S(2)}) copy-start(f32[58]{0:T(128)} %param.12) | copy-start | bytes 700
  78.0 13.1 %copy-start.30 = (s32[64]{0:T(128)S(1)}, s32[64]{0:T(128)}, u32[]{:S(2)}) copy-start(s32[64]{0:T(128)} %param.13) | copy-start | bytes 772
  78.0 126.8 %all-to-all-start.1 = ((f32[16,1,118784]{2,1,0:T(1,128)}), f32[16,1,118784]{2,1,0:T(1,128)}, u32[]{:S(2)}, u32[]{:S(2)}) async-start(f32[16,1,118784]{2,1,0:T(1,128)} %reshape.401), calls=%async_computation.1 | async-start | bytes 15204352 | tf_op jit(solution)/shard_map/all_to_all | solution.py:105
  85.5 93.9 %collective-permute-start = (f32[3,72,1,8]{1,3,2,0:T(8,128)S(1)}, f32[3,72,1,8]{1,3,2,0:T(8,128)S(1)}, u32[]{:S(2)}, u32[]{:S(2)}) collective-permute-start(f32[3,72,1,8]{1,3,2,0:T(8,128)S(1)} %get-tuple-element.232), channel_id=1, source_target_pairs={{8,0},{16,8},{24,16},{32,24},{40,32},{48,40},{56,48},{64,56},{72,6... | collective-permute-start | bytes 20744 | tf_op jit(solution)/shard_map/ppermute | solution.py:21
  90.7 88.7 %collective-permute-start.1 = (f32[3,72,1,8]{1,3,2,0:T(8,128)S(1)}, f32[3,72,1,8]{1,3,2,0:T(8,128)S(1)}, u32[]{:S(2)}, u32[]{:S(2)}) collective-permute-start(f32[3,72,1,8]{1,3,2,0:T(8,128)S(1)} %get-tuple-element.231), channel_id=1, source_target_pairs={{0,8},{8,16},{16,24},{24,32},{32,40},{40,48},{48,56},{56,64},{64,7... | collective-permute-start | bytes 20744 | tf_op jit(solution)/shard_map/ppermute | solution.py:19
  179.4 4.2 copy-start.21
  179.4 4.1 copy-start.23
  180.0 369.1 %collective-permute-start.3 = (f32[3,72,10,1]{1,3,2,0:T(1,128)}, f32[3,72,10,1]{1,3,2,0:T(1,128)}, u32[]{:S(2)}, u32[]{:S(2)}) collective-permute-start(f32[3,72,10,1]{1,3,2,0:T(1,128)} %get-tuple-element.230), channel_id=1, source_target_pairs={{0,1},{1,2},{2,3},{3,4},{4,5},{5,6},{6,7},{7,0},{8,9},{9,10},{10,1... | collective-permute-start | bytes 25928 | tf_op jit(solution)/shard_map/ppermute | solution.py:19
  180.0 369.1 %collective-permute-start.2 = (f32[3,72,10,1]{1,3,2,0:T(1,128)}, f32[3,72,10,1]{1,3,2,0:T(1,128)}, u32[]{:S(2)}, u32[]{:S(2)}) collective-permute-start(f32[3,72,10,1]{1,3,2,0:T(1,128)} %get-tuple-element.229), channel_id=1, source_target_pairs={{1,0},{2,1},{3,2},{4,3},{5,4},{6,5},{7,6},{0,7},{9,8},{10,9},{11,1... | collective-permute-start | bytes 25928 | tf_op jit(solution)/shard_map/ppermute | solution.py:21
  350.5 3.8 copy-start.6
  357.0 2.5 copy-start.11
  366.9 2.6 copy-start.8
  387.8 1.5 copy-start.12
  387.8 2.1 copy-start.13
  392.2 1.5 copy-start.4
  396.0 1.5 copy-start.4
  399.9 1.5 copy-start.4
  403.7 1.5 copy-start.4
  407.5 1.5 copy-start.4
  411.3 1.5 copy-start.4
  415.1 1.5 copy-start.4
  418.9 1.5 copy-start.4
  423.7 2.9 copy-start
  426.6 1.5 copy-start.5
  429.9 1.2 copy-start.1
  431.2 2.9 copy-start
  434.1 1.5 copy-start.5
  437.4 1.2 copy-start.1
  438.6 2.9 copy-start
  441.6 1.5 copy-start.5
  444.8 1.2 copy-start.1
  446.1 2.9 copy-start
  449.0 1.5 copy-start.5
  452.3 1.2 copy-start.1
  453.6 2.9 copy-start
  456.5 1.5 copy-start.5
  461.0 2.9 copy-start
  464.0 1.5 copy-start.5
  467.2 1.2 copy-start.1
  468.5 2.9 copy-start
  471.4 1.5 copy-start.5
  476.0 2.9 copy-start
  478.9 1.5 copy-start.5
  497.0 2.6 copy-start.10
  497.1 3.0 copy-start.2
  506.3 2.1 copy-start.9
  515.2 2.5 copy-start.7
  515.2 3.5 copy-start.16
  515.2 4.0 copy-start.17
  522.3 25.1 %all-to-all-start.3 = ((f32[16,1,928]{2,1,0:T(1,128)}), f32[16,1,928]{2,1,0:T(1,128)S(1)}, u32[]{:S(2)}, u32[]{:S(2)}) async-start(f32[16,1,928]{2,1,0:T(1,128)} %reshape.405), calls=%async_computation.3 | async-start | bytes 131072 | tf_op jit(solution)/shard_map/all_to_all | solution.py:112
  536.7 6.9 %copy-start.3 = (f32[58,64,128]{2,1,0:T(8,128)S(1)}, f32[58,64,128]{2,1,0:T(8,128)}, u32[]{:S(2)}) copy-start(f32[58,64,128]{2,1,0:T(8,128)} %get-tuple-element.77) | copy-start | bytes 5701636
  536.7 6.9 %copy-start.14 = (f32[1,58,64,128]{3,2,1,0:T(8,128)S(1)}, f32[1,58,64,128]{3,2,1,0:T(8,128)}, u32[]{:S(2)}) copy-start(f32[1,58,64,128]{3,2,1,0:T(8,128)} %get-tuple-element.154) | copy-start | bytes 5701636
  536.7 7.1 %copy-start.15 = (f32[58,64,128]{2,1,0:T(8,128)S(1)}, f32[58,64,128]{2,1,0:T(8,128)}, u32[]{:S(2)}) copy-start(f32[58,64,128]{2,1,0:T(8,128)} %get-tuple-element.158) | copy-start | bytes 5701636
  543.8 4.9 copy-start.26
  543.8 5.2 copy-start.28
  543.8 5.2 copy-start.29
  543.8 5.3 copy-start.27
  543.8 5.3 copy-start.19
  543.8 5.3 copy-start.22
  543.8 5.3 copy-start.24
  (3 other events, 3.7 us)
where the time goes:
time: 560 us; the launch traced here: 551 us
  other arithmetic  191 us (34%)
  local copies, waits for them, and re-layouts  191 us (34%)
  waiting for transfers between devices  110 us (20%)
  starting transfers between devices  41.2 us (7%)
  matrix products  14.7 us (3%)
    ppermute x2, waiting for transfers between devices, extended(): lax.ppermute(head, axis, [((i + 1) % count, i) for i in range(count)])  86.5 us
    unnamed x69, local copies, waits for them, and re-layouts  79.7 us
    reduce_sum x2, other arithmetic, cloud_model(): mean_b = jnp.mean(buoy, axis=1, keepdims=True)  75.6 us
    all_to_all x1, other arithmetic, per_device(): lax.all_to_all(sent_state, 'gx', split_axis=3, concat_axis=3, tiled=True)  44 us
    add x16, other arithmetic, sweep(): return press + 0.8 * (rhs_now - applied) / diag_term  28 us
    slice x32, local copies, waits for them, and re-layouts, lap_x(): jnp.roll(field, -1, axis=1)  27.2 us
    while x64, local copies, waits for them, and re-layouts  26.4 us
    all_to_all x1, waiting for transfers between devices, per_device(): lax.all_to_all(sent_state, 'gx', split_axis=3, concat_axis=3, tiled=True)  19.9 us
  transfers between devices with their start and end apart: 8, of which 3 were waited for; matrix products, arithmetic and copies ran while one was open for 66% of the time, Pallas kernels for 0%

commit v1 on v0

v1 whole, which is shorter than its diff:
```python
import jax
import jax.numpy as jnp
from jax import lax
from jax.experimental import pallas as pl
from jax.experimental.pallas import tpu as pltpu
from jax.sharding import PartitionSpec as P

NSTEP = 2
ITERS = 8
GROUPS = 16
RANKS = 8
LANES = 128
HALF = 64
QUAD = 4
OCT = 8
MIB = 1024 * 1024


def spans(start, stop, unroll, body):
    turns = (stop - start) // unroll

    def turn(i, carry):
        body([start + i * unroll + k for k in range(unroll)])
        return carry

    if turns:
        lax.fori_loop(0, turns, turn, 0)
    rest = list(range(start + turns * unroll, stop))
    if rest:
        body(rest)


def lane_ids():
    return lax.broadcasted_iota(jnp.int32, (8, LANES), 1)


def to_column(row, rows):
    n = row.shape[1]
    r = lax.broadcasted_iota(jnp.int32, (rows, n), 0)
    c = lax.broadcasted_iota(jnp.int32, (rows, n), 1)
    return jnp.sum(jnp.where(r == c, jnp.broadcast_to(row, (rows, n)), 0.0), axis=1, keepdims=True)


def slot_tables(owner_row, active_row):
    n = owner_row.shape[1]
    own = owner_row.astype(jnp.float32)
    own_col = to_column(own, n)
    r = lax.broadcasted_iota(jnp.int32, (n, n), 0)
    c = lax.broadcasted_iota(jnp.int32, (n, n), 1)
    before = (own_col == jnp.broadcast_to(own, (n, n))) & (c < r)
    rank = jnp.sum(jnp.where(before, 1.0, 0.0), axis=1, keepdims=True)
    slot = own_col * float(RANKS) + rank
    lanes = lax.broadcasted_iota(jnp.int32, (n, LANES), 1).astype(jnp.float32)
    match = jnp.broadcast_to(slot, (n, LANES)) == lanes
    rows = lax.broadcasted_iota(jnp.int32, (n, LANES), 0).astype(jnp.float32)
    act = jnp.broadcast_to(to_column(active_row.astype(jnp.float32), n), (n, LANES))
    column = jnp.sum(jnp.where(match, rows, 0.0), axis=0, keepdims=True)
    active = jnp.sum(jnp.where(match, act, 0.0), axis=0, keepdims=True)
    return jnp.broadcast_to(column, (8, LANES)), jnp.broadcast_to(active, (8, LANES))


def fill_index(idx_ref, column, offset):
    col = column.astype(jnp.int32)
    for m in range(GROUPS):
        turned = pltpu.roll(col, RANKS * m, 1) if m else col
        idx_ref[m] = turned + offset * ((m // QUAD) % 2)


def group_bits():
    group = lane_ids() // RANKS
    return [((group >> b) & 1) == 1 for b in range(4)]


def barrel(rows, bits):
    rows = [rows[-r % GROUPS] for r in range(GROUPS)]
    for b in range(4):
        step = 1 << b
        rows = [jnp.where(bits[b], rows[(r - step) % GROUPS], rows[r]) for r in range(GROUPS)]
    return rows


def take_lanes(value, index):
    return jnp.take_along_axis(value, index, axis=1, mode="promise_in_bounds")


def turn_by(source, target):
    return lax.rem(source - target + GROUPS, GROUPS) * RANKS


def settle(rows):
    return [pltpu.roll(rows[k], LANES - RANKS * k, 1) if k else rows[k] for k in range(GROUPS)]


def mean_x(v):
    while len(v) > 1:
        v = [a + b for a, b in zip(v[::2], v[1::2])]
    total = jnp.sum(v[0], axis=0, keepdims=True)
    return total * (1.0 / 64.0)


def full_width(ref, source):
    cols, levels = source.shape
    ref[...] = jnp.zeros((LANES, LANES), jnp.float32)
    ref[:cols, :levels] = source
    return jnp.transpose(ref[...])


def early_kernel(
    crm, dyn, owner, active, send,
    raw_b, raw_w, dyn_ref, own_ref, act_ref, square, force_ref, vals, picked, stage, idx_ref, sems, small, out_sems,
):
    nz = raw_b.shape[0]
    cols = raw_b.shape[2]
    levels = dyn_ref.shape[2]
    pairs = nz // 2
    cuts = [0, 5, 11, 17, 23, pairs]
    lots = len(cuts) - 1
    few = [
        pltpu.make_async_copy(s, d, small.at[i])
        for i, (s, d) in enumerate(((dyn, dyn_ref), (owner, own_ref), (active, act_ref)))
    ]
    for copy in few:
        copy.start()
    copies = []
    for i in range(lots):
        part = pl.ds(2 * cuts[i], 2 * (cuts[i + 1] - cuts[i]))
        for f, raw in ((2, raw_b), (1, raw_w)):
            copy = pltpu.make_async_copy(crm.at[f, part], raw.at[part], sems.at[i, f - 1])
            copy.start()
            copies.append(copy)
    for copy in few:
        copy.wait()
    me = lax.axis_index("gx")
    column, active_slots = slot_tables(own_ref[...], act_ref[...])
    fill_index(idx_ref, column, 0)
    after = lax.rem(me + 1, GROUPS)
    for owner_at in range(GROUPS):
        stage[owner_at, pairs] = active_slots
        for f in range(3):
            stage[owner_at, pairs + 1 + f, :, :levels] = jnp.where(
                after == owner_at, dyn_ref[f, cols - 8 :, :], dyn_ref[f, :8, :]
            )
    force_ref[...] = full_width(square, dyn_ref[0])
    act = act_ref[...]
    bits = group_bits()

    def level(zs):
        for z in zs:
            force = force_ref[pl.ds(z, 1), :cols]
            mask = jnp.broadcast_to(z < act, (8, cols))
            b = [raw_b[z, pl.ds(m, 8, stride=8), :] for m in range(OCT)]
            w = [raw_w[z, pl.ds(m, 8, stride=8), :] for m in range(OCT)]
            extra = 0.25 * (force - mean_x(b))
            east = b[1:] + [pltpu.roll(b[0], 7, 0)]
            west = [pltpu.roll(b[-1], 1, 0)] + b[:-1]
            b = [
                jnp.where(mask, (0.6 * b[m] + 0.2 * (east[m] + west[m])) + (extra - 0.5 * w[m]), 0.0)
                for m in range(OCT)
            ]
            extra = 0.25 * (force - mean_x(b))
            east = b[1:] + [pltpu.roll(b[0], 7, 0)]
            west = [pltpu.roll(b[-1], 1, 0)] + b[:-1]
            for m in range(OCT):
                vals[z, m, :, :cols] = (1.1 * b[m] + 0.2 * (east[m] + west[m])) + extra

    def pick(gs):
        for m in range(GROUPS):
            for g in gs:
                picked[g, m] = take_lanes(vals[2 * g + m // OCT, m % OCT], idx_ref[m])

    def pack(gs):
        for g in gs:
            rows = barrel([picked[g, m] for m in range(GROUPS)], bits)
            for owner_at in range(GROUPS):
                stage[owner_at, g] = rows[owner_at]

    stores = []
    for i in range(lots):
        copies[2 * i].wait()
        copies[2 * i + 1].wait()
        spans(2 * cuts[i], 2 * cuts[i + 1], 2, level)
        spans(cuts[i], cuts[i + 1], 2, pick)
        spans(cuts[i], cuts[i + 1], 1, pack)
        stop = cuts[i + 1] if i < lots - 1 else stage.shape[1]
        part = pl.ds(cuts[i], stop - cuts[i])
        copy = pltpu.make_async_copy(stage.at[:, part], send.at[:, part], out_sems.at[i])
        copy.start()
        stores.append(copy)
    for copy in stores:
        copy.wait()


def load_raw(ref, z):
    out = []
    for m in range(QUAD):
        low = ref[z, pl.ds(m, 8, stride=8), :]
        high = ref[z, pl.ds(QUAD + m, 8, stride=8), :]
        out.append(jnp.concatenate([low, high], axis=1))
    return out


def east_of(v, low):
    t = pltpu.roll(v[0], HALF, 1)
    return v[1:] + [jnp.where(low, t, pltpu.roll(t, 7, 0))]


def west_of(v, low):
    t = pltpu.roll(v[QUAD - 1], HALF, 1)
    return [jnp.where(low, pltpu.roll(t, 1, 0), t)] + v[:-1]


def packed_mean(v):
    half = mean_x(v)
    return half + pltpu.roll(half, HALF, 1)


def smooth(v, low):
    return [0.6 * a + 0.2 * (b + c) for a, b, c in zip(v, east_of(v, low), west_of(v, low))]


def twice(value):
    return jnp.where(
        lax.broadcasted_iota(jnp.int32, value.shape, 1) < HALF, value, pltpu.roll(value, HALF, 1)
    )


def sweeps(p_ref, rhs_ref, coef_ref, low):
    nz = p_ref.shape[0]
    zero = [jnp.zeros((8, LANES), jnp.float32)] * QUAD

    def one(step, carry):
        below = zero
        here = [p_ref[0, m] for m in range(QUAD)]
        for z in range(nz):
            above = [p_ref[z + 1, m] for m in range(QUAD)] if z < nz - 1 else zero
            kr, ku, kd = (coef_ref[c, pl.ds(z, 1), :] for c in range(3))
            e, w = east_of(here, low), west_of(here, low)
            for m in range(QUAD):
                new = (0.2 * here[m] + rhs_ref[z, m]) + kr * (e[m] + w[m])
                if z < nz - 1:
                    new = new + ku * above[m]
                if z > 0:
                    new = new + kd * below[m]
                p_ref[z, m] = new
            below, here = here, above
        return carry

    lax.fori_loop(0, ITERS, one, 0)


def fill_coefficients(coef_ref, density_row):
    nz = density_row.shape[1]
    rho = jnp.broadcast_to(to_column(density_row, HALF), (HALF, LANES))
    level = lax.broadcasted_iota(jnp.int32, (HALF, LANES), 0)
    above = pltpu.roll(rho, HALF - 1, 0)
    below = pltpu.roll(rho, 1, 0)
    rho_up = jnp.where(level < nz - 1, 0.5 * (rho + above), 0.0)
    rho_dn = jnp.where(level > 0, pltpu.roll(rho_up, 1, 0), 0.0)
    scale = jnp.where(level < nz, 0.8 / (2.1 * rho + rho_up + rho_dn), 0.0)
    coef_ref[0] = scale * rho
    coef_ref[1] = scale * rho_up
    coef_ref[2] = scale * rho_dn
    coef_ref[3] = -0.5 * scale * rho
    coef_ref[4] = -0.5 * scale * above
    coef_ref[5] = 0.5 * scale * below


def main_kernel(
    crm, dyn_ref, orient_ref, owner_ref, active_ref, density_ref,
    send, tend_ref,
    raw, u_ref, w_ref, b_ref, p_ref, rhs_ref, coef_ref, idx_ref, square, force_ref, picked, sems,
):
    nz = p_ref.shape[0]
    cols = raw.shape[3]
    pairs = nz // 2
    copies = []
    for f in range(4):
        copy = pltpu.make_async_copy(crm.at[f], raw.at[f], sems.at[f])
        copy.start()
        copies.append(copy)
    me = lax.axis_index("gx")
    column, _ = slot_tables(owner_ref[...], active_ref[...])
    fill_index(idx_ref, column, HALF)
    fill_coefficients(coef_ref, density_ref[...])
    first = jnp.concatenate([orient_ref[...], orient_ref[...]], axis=1) == 0
    force_ref[0] = twice(full_width(square, dyn_ref[0]))
    wind = full_width(square, dyn_ref[1])
    force_ref[1] = twice(jnp.where(first, wind, full_width(square, dyn_ref[2])))
    act = jnp.concatenate([active_ref[...], active_ref[...]], axis=1)
    low = lane_ids() < HALF
    bits = group_bits()
    tend_ref[...] = jnp.zeros(tend_ref.shape, jnp.float32)
    for copy in copies:
        copy.wait()

    def prologue(zs):
        done = []
        for z in zs:
            mask = jnp.broadcast_to(z < act, (8, LANES))
            fb, fu = force_ref[0, pl.ds(z, 1), :], force_ref[1, pl.ds(z, 1), :]
            b, w, u, p = (load_raw(raw.at[f], z) for f in (2, 1, 0, 3))
            mean_b, mean_u = packed_mean(b), packed_mean(u)
            extra_b, extra_u = 0.25 * (fb - mean_b), 0.25 * (fu - mean_u)
            new_b = [jnp.where(mask, s + (extra_b - 0.5 * a), 0.0) for s, a in zip(smooth(b, low), w)]
            new_u = [s + extra_u for s in smooth(u, low)]
            done.append((z, mean_b, mean_u, new_b, new_u, [x + y for x, y in zip(w, b)], p))
        for z, mean_b, mean_u, new_b, new_u, new_w, p in done:
            tend_ref[0, pl.ds(z, 1), :] = mean_b
            tend_ref[1, pl.ds(z, 1), :] = mean_u
            for m in range(QUAD):
                b_ref[z, m] = new_b[m]
                u_ref[z, m] = new_u[m]
                w_ref[z, m] = new_w[m]
                p_ref[z, m] = p[m]

    spans(0, nz, 4, prologue)

    def right_side(zs):
        for z in zs:
            up = jnp.minimum(z + 1, nz - 1)
            dn = jnp.maximum(z - 1, 0)
            here, cu, cd = (coef_ref[c, pl.ds(z, 1), :] for c in (3, 4, 5))
            u = [u_ref[z, m] for m in range(QUAD)]
            e, w = east_of(u, low), west_of(u, low)
            for m in range(QUAD):
                rhs_ref[z, m] = here * (e[m] - w[m]) + (cu * w_ref[up, m] + cd * w_ref[dn, m])

    spans(0, nz, 4, right_side)
    sweeps(p_ref, rhs_ref, coef_ref, low)

    def middle(zs):
        done = []
        for z in zs:
            mask = jnp.broadcast_to(z < act, (8, LANES))
            fb, fu = force_ref[0, pl.ds(z, 1), :], force_ref[1, pl.ds(z, 1), :]
            p = [p_ref[z, m] for m in range(QUAD)]
            e, w = east_of(p, low), west_of(p, low)
            up, dn = jnp.minimum(z + 1, nz - 1), jnp.maximum(z - 1, 0)
            top = jnp.where(z < nz - 1, 0.5, 0.0)
            bottom = jnp.where(z > 0, 0.5, 0.0)
            us = [jnp.where(mask, u_ref[z, m] - 0.5 * (e[m] - w[m]), 0.0) for m in range(QUAD)]
            ws = [
                jnp.where(mask, w_ref[z, m] - (top * p_ref[up, m] - bottom * p_ref[dn, m]), 0.0)
                for m in range(QUAD)
            ]
            bs = [b_ref[z, m] for m in range(QUAD)]
            mean_b, mean_u, mean_w = packed_mean(bs), packed_mean(us), packed_mean(ws)
            extra = 0.25 * (fu - mean_u)
            last_b = mean_b + 0.25 * (fb - mean_b) - 0.5 * mean_w
            row = z < act
            tb = (jnp.where(row, last_b, 0.0) - tend_ref[0, pl.ds(z, 1), :]) * (1.0 / NSTEP)
            tu = (jnp.where(row, mean_u + extra, 0.0) - tend_ref[1, pl.ds(z, 1), :]) * (1.0 / NSTEP)
            done.append((z, tb, tu, [s + extra for s in smooth(us, low)], [x + y for x, y in zip(ws, bs)]))
        for z, tb, tu, new_u, new_w in done:
            tend_ref[0, pl.ds(z, 1), :] = tb
            tend_ref[1, pl.ds(z, 1), :] = tu
            for m in range(QUAD):
                u_ref[z, m] = new_u[m]
                b_ref[z, m] = new_w[m]

    spans(0, nz, 4, middle)
    sweeps(p_ref, rhs_ref, coef_ref, low)

    def project(zs):
        for z in zs:
            mask = jnp.broadcast_to(z < act, (8, LANES))
            p = [p_ref[z, m] for m in range(QUAD)]
            e, w = east_of(p, low), west_of(p, low)
            for m in range(QUAD):
                w_ref[z, m] = jnp.where(mask, u_ref[z, m] - 0.5 * (e[m] - w[m]), 0.0)

    spans(0, nz, 4, project)
    for f, source in enumerate((p_ref, b_ref, w_ref)):

        def pick(gs):
            for m in range(GROUPS):
                for g in gs:
                    picked[g, m] = take_lanes(source[2 * g + m // OCT, m % QUAD], idx_ref[m])

        def pack(gs):
            for g in gs:
                rows = barrel([picked[g, m] for m in range(GROUPS)], bits)
                for owner_at in range(GROUPS):
                    send[owner_at, f * pairs + g] = pltpu.roll(rows[owner_at], turn_by(me, owner_at), 1)

        spans(0, pairs, 2, pick)
        spans(0, pairs, 2, pack)


def between_kernel(got, dyn_ref, prev_y, next_y, tend_ref, orient_ref, dyn_out, b_out, act_ref, picked):
    pairs = b_out.shape[0] // 2
    cols, levels = dyn_ref.shape[1:]
    me = lax.axis_index("gx")
    bits = group_bits()
    group = lane_ids() // RANKS
    act = jnp.zeros((8, LANES), jnp.float32)
    for source in range(GROUPS):
        act = jnp.where(group == source, pltpu.roll(got[source, pairs], turn_by(source, me), 1), act)
    act_ref[...] = act

    def turn(gs):
        for g in gs:
            for source in range(GROUPS):
                picked[g, source] = pltpu.roll(got[source, g], turn_by(source, me), 1)

    def place(gs):
        for g in gs:
            rows = settle(barrel([picked[g, source] for source in range(GROUPS)], bits))
            for k in range(GROUPS):
                b_out[2 * g + k // OCT, k % OCT] = rows[k]

    spans(0, pairs, 2, turn)
    spans(0, pairs, 2, place)

    left, right = lax.rem(me + GROUPS - 1, GROUPS), lax.rem(me + 1, GROUPS)
    col = lax.broadcasted_iota(jnp.int32, (cols, levels), 0)
    first_b, last_b = col % 8 == 0, col % 8 == 7
    first = jnp.broadcast_to(to_column(orient_ref[...].astype(jnp.float32), cols), (cols, levels)) < 0.5
    adds = [jnp.transpose(tend_ref[i])[:cols, :levels] for i in range(2)]
    adds = [adds[0], jnp.where(first, adds[1], 0.0), jnp.where(first, 0.0, adds[1])]

    def turned(value, by):
        by = by % cols
        return jnp.concatenate([value[cols - by :], value[: cols - by]], axis=0)

    for f in range(3):
        here = dyn_ref[f]
        up_x = jnp.concatenate([got[left, pairs + 1 + f][:, :levels], here[: cols - 8]], axis=0)
        dn_x = jnp.concatenate([here[8:], got[right, pairs + 1 + f][:, :levels]], axis=0)
        up_y = jnp.where(first_b, turned(prev_y[f], -7), turned(here, 1))
        dn_y = jnp.where(last_b, turned(next_y[f], 7), turned(here, -1))
        dyn_out[f] = (here + 0.2 * ((up_x + dn_x) + (up_y + dn_y) - 4.0 * here)) + adds[f]


def last_kernel(got, b_ref, act_ref, out, pressure, stage, out_sems):
    nz = stage.shape[1]
    pairs = nz // 2
    cuts = [0, 6, 12, 18, 24, pairs]
    ahead = [0, 8, 14, 20, 26, pairs]
    lots = len(cuts) - 1
    bits = group_bits()
    act = act_ref[...]
    full = act > 0.0
    for m in range(OCT):
        pressure[0, m] = jnp.zeros((8, LANES), jnp.float32)
        pressure[nz + 1, m] = jnp.zeros((8, LANES), jnp.float32)

    def unpack(f, g):
        return settle(barrel([got[source, f * pairs + g] for source in range(GROUPS)], bits))

    def take_p(gs):
        for g in gs:
            rows = unpack(0, g)
            for k in range(GROUPS):
                z, m = 2 * g + k // OCT, k % OCT
                value = jnp.where(full, rows[k], 0.0)
                pressure[z + 1, m] = value
                stage[3, z, pl.ds(m, 8, stride=8), :] = value

    def take_rest(gs):
        for g in gs:
            w, u = unpack(1, g), unpack(2, g)
            for k in range(GROUPS):
                z, m = 2 * g + k // OCT, k % OCT
                level = z if isinstance(z, int) else z.astype(jnp.float32)
                mask = level < act
                row = pl.ds(m, 8, stride=8)
                gradient = pressure[z + 2, m] - pressure[z, m]
                stage[0, z, row, :] = jnp.where(full, u[k], 0.0)
                stage[1, z, row, :] = jnp.where(mask, w[k] - 0.5 * gradient, 0.0)
                stage[2, z, row, :] = jnp.where(mask, b_ref[z, m] - 0.5 * w[k], 0.0)

    stores = []
    for i in range(lots):
        spans(ahead[i], ahead[i + 1], 2, take_p)
        spans(cuts[i], cuts[i + 1], 2, take_rest)
        part = pl.ds(2 * cuts[i], 2 * (cuts[i + 1] - cuts[i]))
        for f in range(4):
            copy = pltpu.make_async_copy(stage.at[f, part], out.at[f, part], out_sems.at[i, f])
            copy.start()
            stores.append(copy)
    for copy in stores:
        copy.wait()


def per_device(dynamics, crm_state, density, orientation, owner, active):
    nz, nx, cols = crm_state.shape[1:]
    levels = dynamics.shape[1]
    pairs = nz // 2
    f32 = jnp.float32
    vmem = pl.BlockSpec(memory_space=pltpu.VMEM)
    hbm = pl.BlockSpec(memory_space=pltpu.HBM)
    shape = jax.ShapeDtypeStruct
    dma = pltpu.SemaphoreType.DMA
    square = pltpu.VMEM((LANES, LANES), f32)
    index = pltpu.VMEM((GROUPS, 8, LANES), jnp.int32)
    turned = jnp.swapaxes(dynamics, 1, 2)
    owner_row, active_row, orient_row = owner[None], active[None], orientation[None]
    density_row = density[None]
    state_in = pltpu.with_memory_space_constraint(crm_state, pltpu.HBM)

    def params(mib):
        return pltpu.CompilerParams(vmem_limit_bytes=mib * MIB)

    def neighbour(field, axis, by):
        count = lax.axis_size(axis)
        return lax.ppermute(field, axis, [(i, (i + by) % count) for i in range(count)])

    send_b = pl.pallas_call(
        early_kernel,
        out_shape=pltpu.HBM((GROUPS, pairs + 4, 8, LANES), f32),
        in_specs=[hbm] * 4,
        out_specs=hbm,
        scratch_shapes=[
            pltpu.VMEM((nz, nx, cols), f32),
            pltpu.VMEM((nz, nx, cols), f32),
            pltpu.VMEM((3, cols, levels), f32),
            pltpu.VMEM((1, cols), jnp.int32),
            pltpu.VMEM((1, cols), jnp.int32),
            square,
            square,
            pltpu.VMEM((nz, OCT, 8, LANES), f32),
            pltpu.VMEM((pairs, GROUPS, 8, LANES), f32),
            pltpu.VMEM((GROUPS, pairs + 4, 8, LANES), f32),
            index,
            dma((5, 2)),
            dma((3,)),
            dma((5,)),
        ],
        compiler_params=params(16),
        name="early_buoyancy",
    )(state_in, *(pltpu.with_memory_space_constraint(x, pltpu.HBM) for x in (turned, owner_row, active_row)))
    got_b = lax.all_to_all(send_b, "gx", 0, 0, tiled=True)

    state = pltpu.VMEM((nz, QUAD, 8, LANES), f32)
    send, tends = pl.pallas_call(
        main_kernel,
        out_shape=[shape((GROUPS, 3 * pairs, 8, LANES), f32), shape((2, LANES, LANES), f32)],
        in_specs=[hbm, vmem, vmem, vmem, vmem, vmem],
        out_specs=[vmem, vmem],
        scratch_shapes=[pltpu.VMEM((4, nz, nx, cols), f32)]
        + [state] * 5
        + [
            pltpu.VMEM((6, HALF, LANES), f32),
            index,
            square,
            pltpu.VMEM((2, LANES, LANES), f32),
            pltpu.VMEM((pairs, GROUPS, 8, LANES), f32),
            dma((4,)),
        ],
        compiler_params=params(20),
        cost_estimate=pl.CostEstimate(flops=60_000_000, bytes_accessed=14_000_000, transcendentals=0),
        name="cloud_steps",
    )(state_in, turned, orient_row, owner_row, active_row, density_row)
    prev_y, next_y = neighbour(turned, "gy", 1), neighbour(turned, "gy", -1)
    dynamics_next, placed_b, act = pl.pallas_call(
        between_kernel,
        out_shape=[
            shape(turned.shape, f32),
            shape((nz, OCT, 8, LANES), f32),
            shape((8, LANES), f32),
        ],
        in_specs=[vmem] * 6,
        out_specs=[vmem, vmem, vmem],
        scratch_shapes=[pltpu.VMEM((pairs, GROUPS, 8, LANES), f32)],
        compiler_params=params(16),
        name="dynamics_and_b",
    )(got_b, turned, prev_y, next_y, tends, orient_row)

    send, dynamics_next, placed_b, act = lax.optimization_barrier((send, dynamics_next, placed_b, act))
    got = lax.all_to_all(send, "gx", 0, 0, tiled=True)

    crm_next = pl.pallas_call(
        last_kernel,
        out_shape=pltpu.HBM((4, nz, nx, LANES), f32),
        in_specs=[vmem, vmem, vmem],
        out_specs=hbm,
        scratch_shapes=[
            pltpu.VMEM((nz + 2, OCT, 8, LANES), f32),
            pltpu.VMEM((4, nz, nx, LANES), f32),
            dma((5, 4)),
        ],
        compiler_params=params(12),
        name="place_state",
    )(got, placed_b, act)
    return (jnp.swapaxes(dynamics_next, 1, 2), crm_next)


def solution(mesh):
    in_specs = (
        P(None, None, ("gx", "gy")),
        P(None, None, None, ("gx", "gy")),
        P(),
        P(("gx", "gy")),
        P(("gx", "gy")),
        P(("gx", "gy")),
    )
    out_specs = (P(None, None, ("gx", "gy")), P(None, None, None, ("gx", "gy")))
    return jax.shard_map(
        per_device, mesh=mesh, in_specs=in_specs, out_specs=out_specs, check_vma=False
    )
```

time: 560 us -> 132 us (0.24); the launches traced: 551 us -> 132 us
  other arithmetic: 191 us -> 0 us
  local copies, waits for them, and re-layouts: 191 us -> 2.52 us
  waiting for transfers between devices: 110 us -> 0.01 us
  blocking collectives: 0 us -> 73.2 us
  Pallas kernels: 0 us -> 44.8 us
  starting transfers between devices: 41.2 us -> 10.3 us
  matrix products: 14.7 us -> 0 us
    ppermute x4 -> x2, waiting for transfers between devices: 86.5 us -> 0.01 us  [neighbour(): lax.ppermute(field, axis, [(i, (i + by) % count) for i in range(count)])]
    reduce_sum x5 -> x0, other arithmetic: 85.3 us -> none  [the longest x2 75.6 us: cloud_model(): mean_b = jnp.mean(buoy, axis=1, keepdims=True)]
    unnamed x69 -> x12, local copies, waits for them, and re-layouts: 79.7 us -> 2.52 us
    all_to_all x0 -> x1, blocking collectives: none -> 73.2 us  [per_device(): got = lax.all_to_all(send, 'gx', 0, 0, tiled=True)]
    slice x61 -> x0, local copies, waits for them, and re-layouts: 48.2 us -> none  [the longest x32 27.2 us: lap_x(): jnp.roll(field, -1, axis=1)]
    all_to_all x4 -> x0, other arithmetic: 46.6 us -> none  [the longest x1 44 us: per_device(): lax.all_to_all(sent_state, 'gx', split_axis=3, concat_axis=3, tiled=True)]
    pallas_call x0 -> x4, Pallas kernels: none -> 44.8 us  [the longest x1 28 us: per_device(): pl.pallas_call(main_kernel, out_shape=[shape((GROUPS, 3 * pairs, 8, LANES...]
    add x20 -> x0, other arithmetic: 34.7 us -> none  [the longest x16 28 us: sweep(): return press + 0.8 * (rhs_now - applied) / diag_term]
  transfers between devices with their start and end apart: 8 -> 3, of which waited for: 3 -> 0; matrix products, arithmetic and copies ran while one was open for 66% -> 0% of each run, Pallas kernels for 0% -> 21%
where the time goes in v1:
time: 132 us
  blocking collectives  73.2 us (55%)
  Pallas kernels  44.8 us (34%)
  starting transfers between devices  10.3 us (8%)
  local copies, waits for them, and re-layouts  2.52 us (2%)
    all_to_all x1, blocking collectives, per_device(): got = lax.all_to_all(send, 'gx', 0, 0, tiled=True)  73.2 us
    pallas_call x1, Pallas kernels, per_device(): pl.pallas_call(main_kernel, out_shape=[shape((GROUPS, 3 * pairs, 8, LANES...  28 us
    pallas_call x1, Pallas kernels, per_device(): pl.pallas_call(early_kernel, out_shape=pltpu.HBM((GROUPS, pairs + 4, 8, L...  8.28 us
    all_to_all x1, starting transfers between devices, per_device(): got_b = lax.all_to_all(send_b, 'gx', 0, 0, tiled=True)  7.13 us
    pallas_call x1, Pallas kernels, per_device(): pl.pallas_call(last_kernel, out_shape=pltpu.HBM((4, nz, nx, LANES), f32),...  4.76 us
    pallas_call x1, Pallas kernels, per_device(): pl.pallas_call(between_kernel, out_shape=[shape(turned.shape, f32), shape...  3.76 us
    ppermute x2, starting transfers between devices, neighbour(): lax.ppermute(field, axis, [(i, (i + by) % count) for i in range(count)])  3.21 us
  transfers between devices with their start and end apart: 3, of which 0 were waited for; matrix products, arithmetic and copies ran while one was open for 0% of the time, Pallas kernels for 21%

profile of v1, /device:TPU:0, one launch (start us, length us, event | category | flops | bytes accessed | tf_op | source)
XLA Modules:
  0.0 131.6 jit_solution(16764510696507827870)
XLA Ops:
  0.6 0.0 copy-start.1
  0.6 0.0 copy-start.2
  0.7 0.0 copy-start.3
  0.7 0.0 copy-start.4
  0.7 0.0 copy-start.5
  0.7 8.3 %early_buoyancy.1 = f32[16,33,8,128]{3,2,1,0:T(8,128)} custom-call(f32[4,58,64,64]{3,2,1,0:T(8,128)} %crm.3, f32[3,64,72]{2,1,0:T(8,128)} %bitcast.6, s32[1,64]{1,0:T(1,128)} %bitcast.11, s32[1,64]{1,0:T(1,128)} %bitcast.13), custom_call_target="tpu_custom_call" | custom-call | tf_op jit(solution)/shard_map/early_buoyancy/pallas_call | solution.py:509
  9.0 7.1 %all-to-all-start = ((f32[16,33,8,128]{3,2,1,0:T(8,128)}), f32[16,33,8,128]{3,2,1,0:T(8,128)S(1)}, u32[]{:S(2)}, u32[]{:S(2)}) async-start(f32[16,33,8,128]{3,2,1,0:T(8,128)} %early_buoyancy.1), calls=%async_computation | async-start | bytes 4325376 | tf_op jit(solution)/shard_map/all_to_all | solution.py:533
  16.1 0.0 copy-done.1
  16.1 3.2 %collective-permute-start.1 = (f32[3,64,72]{2,1,0:T(8,128)S(1)}, f32[3,64,72]{2,1,0:T(8,128)S(1)}, u32[]{:S(2)}, u32[]{:S(2)}) collective-permute-start(f32[3,64,72]{2,1,0:T(8,128)S(1)} %bitcast.7), channel_id=1, source_target_pairs={{0,7},{1,0},{2,1},{3,2},{4,3},{5,4},{6,5},{7,6},{8,15},{9,8},{10,9... | collective-permute-start | bytes 165896 | tf_op jit(solution)/shard_map/ppermute | solution.py:507
  19.3 0.0 collective-permute-start
  19.3 0.0 copy-done.2
  19.3 0.0 copy-done.3
  19.3 0.0 copy-done.4
  19.4 0.0 copy-done.5
  19.4 28.0 %cloud_steps.1 = (f32[16,87,8,128]{3,2,1,0:T(8,128)S(1)}, f32[2,128,128]{2,1,0:T(8,128)S(1)}) custom-call(f32[4,58,64,64]{3,2,1,0:T(8,128)} %crm.3, f32[3,64,72]{2,1,0:T(8,128)S(1)} %bitcast.9, s32[1,64]{1,0:T(1,128)S(1)} %bitcast.15, s32[1,64]{1,0:T(1,128)S(1)} %bitcast.12, s32[1,64]{1,0:T(1,128)S(1)} %bitcast.14, f32[1,58]{1,0:T(1,128)S(1)} %bitcast.17), custom_call_target="tpu_custom_call" | custom-call | flops 60000000 | bytes 14000000 | tf_op jit(solution)/shard_map/cloud_steps/pallas_call | solution.py:536
  47.4 0.0 copy-start
  47.4 2.5 %copy-done = f32[16,87,8,128]{3,2,1,0:T(8,128)} copy-done((f32[16,87,8,128]{3,2,1,0:T(8,128)}, f32[16,87,8,128]{3,2,1,0:T(8,128)S(1)}, u32[]{:S(2)}) %copy-start) | copy-done | bytes 5701656
  49.9 0.0 collective-permute-done.1.next_y
  49.9 0.0 collective-permute-done.prev_y
  49.9 0.0 all-to-all-done.got
  49.9 3.8 %dynamics_and_b.1 = (f32[3,64,72]{2,1,0:T(8,128)}, f32[58,8,8,128]{3,2,1,0:T(8,128)S(1)}, f32[8,128]{1,0:T(8,128)S(1)}) custom-call(f32[16,33,8,128]{3,2,1,0:T(8,128)S(1)} %all-to-all-done.got, f32[3,64,72]{2,1,0:T(8,128)S(1)} %bitcast.10, f32[3,64,72]{2,1,0:T(8,128)S(1)} %collective-permute-done.prev_y, f32[3,64,72]{2,1,0:T(8,128)S(1)} %collective-permute-done.1.next_y, ...), custom_call_target="tpu_custom_call" | custom-call | tf_op jit(solution)/shard_map/dynamics_and_b/pallas_call | solution.py:556
  53.7 73.2 %all_to_all.10.got = f32[16,87,8,128]{3,2,1,0:T(8,128)S(1)} all-to-all(f32[16,87,8,128]{3,2,1,0:T(8,128)} %copy-done), channel_id=1, replica_groups=mesh['gx'=16,'gy'=8] {'gx'}, dimensions={0} | all-to-all | bytes 11403264 | tf_op jit(solution)/shard_map/all_to_all | solution.py:571
  126.9 4.8 %place_state.1 = f32[4,58,64,128]{3,2,1,0:T(8,128)} custom-call(f32[16,87,8,128]{3,2,1,0:T(8,128)S(1)} %all_to_all.10.got, f32[58,8,8,128]{3,2,1,0:T(8,128)S(1)} %get-tuple-element.18.b_ref, f32[8,128]{1,0:T(8,128)S(1)} %get-tuple-element.19.act_ref), custom_call_target="tpu_custom_call" | custom-call | tf_op jit(solution)/shard_map/place_state/pallas_call | solution.py:573
Async XLA Ops:
  0.6 15.5 %copy-start.1 = (f32[3,72,64]{1,2,0:T(8,128)S(1)}, f32[3,72,64]{1,2,0:T(8,128)}, u32[]{:S(2)}) copy-start(f32[3,72,64]{1,2,0:T(8,128)} %param.6) | copy-start | bytes 165892
  0.6 18.7 %copy-start.2 = (s32[64]{0:T(128)S(1)}, s32[64]{0:T(128)}, u32[]{:S(2)}) copy-start(s32[64]{0:T(128)} %param.10) | copy-start | bytes 772
  0.7 18.7 %copy-start.3 = (s32[64]{0:T(128)S(1)}, s32[64]{0:T(128)}, u32[]{:S(2)}) copy-start(s32[64]{0:T(128)} %param.11) | copy-start | bytes 772
  0.7 18.7 %copy-start.4 = (s32[64]{0:T(128)S(1)}, s32[64]{0:T(128)}, u32[]{:S(2)}) copy-start(s32[64]{0:T(128)} %param.9) | copy-start | bytes 772
  0.7 18.7 %copy-start.5 = (f32[58]{0:T(128)S(1)}, f32[58]{0:T(128)}, u32[]{:S(2)}) copy-start(f32[58]{0:T(128)} %param.8) | copy-start | bytes 700
  9.0 40.9 %all-to-all-start = ((f32[16,33,8,128]{3,2,1,0:T(8,128)}), f32[16,33,8,128]{3,2,1,0:T(8,128)S(1)}, u32[]{:S(2)}, u32[]{:S(2)}) async-start(f32[16,33,8,128]{3,2,1,0:T(8,128)} %early_buoyancy.1), calls=%async_computation | async-start | bytes 4325376 | tf_op jit(solution)/shard_map/all_to_all | solution.py:533
  16.1 33.8 %collective-permute-start.1 = (f32[3,64,72]{2,1,0:T(8,128)S(1)}, f32[3,64,72]{2,1,0:T(8,128)S(1)}, u32[]{:S(2)}, u32[]{:S(2)}) collective-permute-start(f32[3,64,72]{2,1,0:T(8,128)S(1)} %bitcast.7), channel_id=1, source_target_pairs={{0,7},{1,0},{2,1},{3,2},{4,3},{5,4},{6,5},{7,6},{8,15},{9,8},{10,9... | collective-permute-start | bytes 165896 | tf_op jit(solution)/shard_map/ppermute | solution.py:507
  19.3 30.6 %collective-permute-start = (f32[3,64,72]{2,1,0:T(8,128)S(1)}, f32[3,64,72]{2,1,0:T(8,128)S(1)}, u32[]{:S(2)}, u32[]{:S(2)}) collective-permute-start(f32[3,64,72]{2,1,0:T(8,128)S(1)} %bitcast.8), channel_id=1, source_target_pairs={{0,1},{1,2},{2,3},{3,4},{4,5},{5,6},{6,7},{7,0},{8,9},{9,10},{10,1... | collective-permute-start | bytes 165896 | tf_op jit(solution)/shard_map/ppermute | solution.py:507
  47.4 2.5 %copy-start = (f32[16,87,8,128]{3,2,1,0:T(8,128)}, f32[16,87,8,128]{3,2,1,0:T(8,128)S(1)}, u32[]{:S(2)}) copy-start(f32[16,87,8,128]{3,2,1,0:T(8,128)S(1)} %get-tuple-element.17) | copy-start | bytes 17104900

commit v2 on v1

v2 whole, which is shorter than its diff:
```python
import jax
import jax.numpy as jnp
from jax import lax
from jax.experimental import pallas as pl
from jax.experimental.pallas import tpu as pltpu
from jax.sharding import PartitionSpec as P

NSTEP = 2
ITERS = 8
GROUPS = 16
RANKS = 8
LANES = 128
HALF = 64
QUAD = 4
OCT = 8
TAIL = 88
MIB = 1024 * 1024


def spans(start, stop, unroll, body):
    turns = (stop - start) // unroll

    def turn(i, carry):
        body([start + i * unroll + k for k in range(unroll)])
        return carry

    if turns:
        lax.fori_loop(0, turns, turn, 0)
    rest = list(range(start + turns * unroll, stop))
    if rest:
        body(rest)


def lane_ids():
    return lax.broadcasted_iota(jnp.int32, (8, LANES), 1)


def to_column(row, rows):
    n = row.shape[1]
    r = lax.broadcasted_iota(jnp.int32, (rows, n), 0)
    c = lax.broadcasted_iota(jnp.int32, (rows, n), 1)
    return jnp.sum(jnp.where(r == c, jnp.broadcast_to(row, (rows, n)), 0.0), axis=1, keepdims=True)


def slot_tables(owner_row, active_row):
    n = owner_row.shape[1]
    own = owner_row.astype(jnp.float32)
    own_col = to_column(own, n)
    r = lax.broadcasted_iota(jnp.int32, (n, n), 0)
    c = lax.broadcasted_iota(jnp.int32, (n, n), 1)
    before = (own_col == jnp.broadcast_to(own, (n, n))) & (c < r)
    rank = jnp.sum(jnp.where(before, 1.0, 0.0), axis=1, keepdims=True)
    slot = own_col * float(RANKS) + rank
    lanes = lax.broadcasted_iota(jnp.int32, (n, LANES), 1).astype(jnp.float32)
    match = jnp.broadcast_to(slot, (n, LANES)) == lanes
    act = jnp.broadcast_to(to_column(active_row.astype(jnp.float32), n), (n, LANES))
    active = jnp.sum(jnp.where(match, act, 0.0), axis=0, keepdims=True)
    return jnp.where(match, 1.0, 0.0), jnp.broadcast_to(active, (8, LANES))


def in_three(value):
    high = value.astype(jnp.bfloat16)
    rest = value - high.astype(jnp.float32)
    middle = rest.astype(jnp.bfloat16)
    low = (rest - middle.astype(jnp.float32)).astype(jnp.bfloat16)
    return jnp.concatenate([high, middle, low], axis=1)


def to_slots(value, match_ref):
    return jnp.dot(in_three(value), match_ref[...], preferred_element_type=jnp.float32)


def group_bits():
    group = lane_ids() // RANKS
    return [((group >> b) & 1) == 1 for b in range(4)]


def barrel(rows, bits):
    rows = [rows[-r % GROUPS] for r in range(GROUPS)]
    for b in range(4):
        step = 1 << b
        rows = [jnp.where(bits[b], rows[(r - step) % GROUPS], rows[r]) for r in range(GROUPS)]
    return rows


def peer(j, me):
    return lax.rem(j - me + GROUPS, GROUPS)


def mean_x(v):
    while len(v) > 1:
        v = [a + b for a, b in zip(v[::2], v[1::2])]
    total = jnp.sum(v[0], axis=0, keepdims=True)
    return total * (1.0 / 64.0)


def full_width(ref, source):
    cols, levels = source.shape
    ref[...] = jnp.zeros((LANES, LANES), jnp.float32)
    ref[:cols, :levels] = source
    return jnp.transpose(ref[...])


def edge_rows(fields, lane, levels):
    spare = LANES - levels
    row_a = jnp.where(lane < levels, fields[0], pltpu.roll(fields[1], levels, 1))
    row_b = jnp.where(lane < levels, fields[2], pltpu.roll(fields[1], levels - spare, 1))
    return row_a, row_b


def edge_fields(row_a, row_b, lane, levels):
    spare = LANES - levels
    middle = jnp.where(
        lane < spare, pltpu.roll(row_a, spare, 1), pltpu.roll(row_b, LANES - levels + spare, 1)
    )
    return row_a, middle, row_b


def early_kernel(
    crm, dyn, owner, active, send,
    raw_b, raw_w, dyn_ref, wide_ref, own_ref, act_ref, square, force_ref, vals, placed, stage, idx_ref, sems, small, out_sems,
):
    nz = raw_b.shape[0]
    cols = raw_b.shape[2]
    levels = dyn_ref.shape[2]
    pairs = nz // 2
    turns = [0, 3, 6, 9, 12, (pairs + 1) // 2 + 2]
    cuts = [4 * t for t in turns[:-1]] + [nz]
    lots = len(cuts) - 1
    few = [
        pltpu.make_async_copy(s, d, small.at[i])
        for i, (s, d) in enumerate(((dyn, dyn_ref), (owner, own_ref), (active, act_ref)))
    ]
    for copy in few:
        copy.start()
    copies = []
    for i in range(lots):
        part = pl.ds(cuts[i], cuts[i + 1] - cuts[i])
        copies.append(
            [
                pltpu.make_async_copy(crm.at[f, part], raw.at[part], sems.at[i, f - 1])
                for f, raw in ((2, raw_b), (1, raw_w))
            ]
        )
    for lot in copies[:2]:
        for copy in lot:
            copy.start()
    for copy in few:
        copy.wait()
    me = lax.axis_index("gx")
    match, active_slots = slot_tables(own_ref[...], act_ref[...])
    rows = lax.broadcasted_iota(jnp.int32, match.shape, 0).astype(jnp.float32)
    column = jnp.broadcast_to(jnp.sum(match * rows, axis=0, keepdims=True), (8, LANES)).astype(jnp.int32)
    for m in range(GROUPS):
        idx_ref[m] = pltpu.roll(column, lax.rem(me + m, GROUPS) * RANKS, 1)
    after = lax.rem(me + 1, GROUPS)
    wide_ref[:, :, :levels] = dyn_ref[...]
    lane = lane_ids()
    edges = [edge_rows([wide_ref[f, pl.ds(at, 8), :] for f in range(3)], lane, levels) for at in (0, cols - 8)]
    for owner_at in range(GROUPS):
        row_a, row_b = (jnp.where(after == owner_at, far, near) for near, far in zip(*edges))
        ranks = pltpu.roll(active_slots, (TAIL + LANES - RANKS * owner_at) % LANES, 1)
        stage[owner_at, pairs] = row_a
        stage[owner_at, pairs + 1] = jnp.where(lane < TAIL, row_b, ranks)
    force_ref[...] = full_width(square, dyn_ref[0])
    act = act_ref[...]
    bits = group_bits()

    def level(zs):
        for z in zs:
            force = force_ref[pl.ds(z, 1), :cols]
            mask = jnp.broadcast_to(z < act, (8, cols))
            b = [raw_b[z, pl.ds(m, 8, stride=8), :] for m in range(OCT)]
            w = [raw_w[z, pl.ds(m, 8, stride=8), :] for m in range(OCT)]
            extra = 0.25 * (force - mean_x(b))
            east = b[1:] + [pltpu.roll(b[0], 7, 0)]
            west = [pltpu.roll(b[-1], 1, 0)] + b[:-1]
            b = [
                jnp.where(mask, (0.6 * b[m] + 0.2 * (east[m] + west[m])) + (extra - 0.5 * w[m]), 0.0)
                for m in range(OCT)
            ]
            extra = 0.25 * (force - mean_x(b))
            east = b[1:] + [pltpu.roll(b[0], 7, 0)]
            west = [pltpu.roll(b[-1], 1, 0)] + b[:-1]
            for m in range(OCT):
                vals[z, m, :, :cols] = (1.1 * b[m] + 0.2 * (east[m] + west[m])) + extra

    def step(t, carry):
        for half in range(2):
            first, second, third = (jnp.clip(2 * (t - k) + half, 0, pairs - 1) for k in range(3))
            slots = [
                jnp.take_along_axis(
                    vals[2 * second + m // OCT, m % OCT], idx_ref[m], axis=1, mode="promise_in_bounds"
                )
                for m in range(GROUPS)
            ]
            level([2 * first, 2 * first + 1])
            rows = barrel([placed[third, m] for m in range(GROUPS)], bits)
            for j in range(GROUPS):
                stage[peer(j, me), third] = rows[j]
            for m in range(GROUPS):
                placed[second, m] = slots[m]
        return carry

    stores = []
    for i in range(lots):
        for copy in copies[i]:
            copy.wait()
        for lot in copies[i + 2 : i + 3]:
            for copy in lot:
                copy.start()
        lax.fori_loop(turns[i], turns[i + 1], step, 0)
        start = max(2 * (turns[i] - 2), 0)
        stop = 2 * (turns[i + 1] - 2) if i < lots - 1 else stage.shape[1]
        part = pl.ds(start, stop - start)
        copy = pltpu.make_async_copy(stage.at[:, part], send.at[:, part], out_sems.at[i])
        copy.start()
        stores.append(copy)
    for copy in stores:
        copy.wait()


def load_rows(ref, z):
    return [ref[z, pl.ds(m, 8, stride=8), :] for m in range(OCT)]


def side_by_side(v):
    return [jnp.concatenate([v[m], v[QUAD + m]], axis=1) for m in range(QUAD)]


def smooth_rows(v):
    east = v[1:] + [pltpu.roll(v[0], 7, 0)]
    west = [pltpu.roll(v[-1], 1, 0)] + v[:-1]
    return [0.6 * a + 0.2 * (b + c) for a, b, c in zip(v, east, west)]


def east_of(v, low):
    t = pltpu.roll(v[0], HALF, 1)
    return v[1:] + [jnp.where(low, t, pltpu.roll(t, 7, 0))]


def west_of(v, low):
    t = pltpu.roll(v[QUAD - 1], HALF, 1)
    return [jnp.where(low, pltpu.roll(t, 1, 0), t)] + v[:-1]


def packed_mean(v):
    half = mean_x(v)
    return half + pltpu.roll(half, HALF, 1)


def smooth(v, low):
    return [0.6 * a + 0.2 * (b + c) for a, b, c in zip(v, east_of(v, low), west_of(v, low))]


def twice(value):
    return jnp.where(
        lax.broadcasted_iota(jnp.int32, value.shape, 1) < HALF, value, pltpu.roll(value, HALF, 1)
    )


def sweeps(p_ref, rhs_ref, coef_ref, low, nz):
    zero = [jnp.zeros((8, LANES), jnp.float32)] * QUAD

    def one(step, carry):
        below = zero
        here = [p_ref[0, m] for m in range(QUAD)]
        for z in range(nz):
            above = [p_ref[z + 1, m] for m in range(QUAD)] if z < nz - 1 else zero
            kr, ku, kd = (coef_ref[c, pl.ds(z, 1), :] for c in range(3))
            e, w = east_of(here, low), west_of(here, low)
            for m in range(QUAD):
                new = (0.2 * here[m] + rhs_ref[z, m]) + kr * (e[m] + w[m])
                if z < nz - 1:
                    new = new + ku * above[m]
                if z > 0:
                    new = new + kd * below[m]
                p_ref[z, m] = new
            below, here = here, above
        return carry

    lax.fori_loop(0, ITERS, one, 0)


def fill_coefficients(coef_ref, density_row):
    nz = density_row.shape[1]
    rho = jnp.broadcast_to(to_column(density_row, HALF), (HALF, LANES))
    level = lax.broadcasted_iota(jnp.int32, (HALF, LANES), 0)
    above = pltpu.roll(rho, HALF - 1, 0)
    below = pltpu.roll(rho, 1, 0)
    rho_up = jnp.where(level < nz - 1, 0.5 * (rho + above), 0.0)
    rho_dn = jnp.where(level > 0, pltpu.roll(rho_up, 1, 0), 0.0)
    scale = jnp.where(level < nz, 0.8 / (2.1 * rho + rho_up + rho_dn), 0.0)
    coef_ref[0] = scale * rho
    coef_ref[1] = scale * rho_up
    coef_ref[2] = scale * rho_dn
    coef_ref[3] = -0.5 * scale * rho
    coef_ref[4] = -0.5 * scale * above
    coef_ref[5] = 0.5 * scale * below


def main_kernel(
    crm, dyn_ref, orient_ref, owner_ref, active_ref, density_ref,
    send, tend_ref,
    raw, u_ref, w_ref, b_ref, p_ref, rhs_ref, coef_ref, match_ref, square, force_ref, placed, stage, sems, out_sems,
):
    nz = raw.shape[1]
    cols = raw.shape[3]
    pairs = nz // 2
    cuts = [0, 12, 28, 44, nz]
    copies = []
    for i in range(4):
        part = pl.ds(cuts[i], cuts[i + 1] - cuts[i])
        for f in range(4):
            copy = pltpu.make_async_copy(crm.at[f, part], raw.at[f, part], sems.at[i, f])
            copy.start()
            copies.append(copy)
    me = lax.axis_index("gx")
    match, _ = slot_tables(owner_ref[...], active_ref[...])
    match_ref[...] = jnp.zeros(match_ref.shape, jnp.bfloat16)
    for part in range(3):
        for half in range(2):
            at = part * LANES + half * HALF
            match_ref[at : at + HALF, half * LANES : half * LANES + LANES] = match.astype(jnp.bfloat16)
    shifts = [lax.rem(me + m, GROUPS) * RANKS for m in range(GROUPS)]
    fill_coefficients(coef_ref, density_ref[...])
    first = jnp.concatenate([orient_ref[...], orient_ref[...]], axis=1) == 0
    force_ref[0] = twice(full_width(square, dyn_ref[0]))
    wind = full_width(square, dyn_ref[1])
    force_ref[1] = twice(jnp.where(first, wind, full_width(square, dyn_ref[2])))
    narrow = active_ref[...]
    act = jnp.concatenate([narrow, narrow], axis=1)
    low = lane_ids() < HALF
    bits = group_bits()
    tend_ref[...] = jnp.zeros(tend_ref.shape, jnp.float32)

    def prologue(zs):
        for z in zs:
            mask = jnp.broadcast_to(z < narrow, (8, cols))
            fb, fu = force_ref[0, pl.ds(z, 1), :cols], force_ref[1, pl.ds(z, 1), :cols]
            b, w, u, p = (load_rows(raw.at[f], z) for f in (2, 1, 0, 3))
            mean_b, mean_u = mean_x(b), mean_x(u)
            extra_b, extra_u = 0.25 * (fb - mean_b), 0.25 * (fu - mean_u)
            new_b = [jnp.where(mask, s + (extra_b - 0.5 * a), 0.0) for s, a in zip(smooth_rows(b), w)]
            new_u = [s + extra_u for s in smooth_rows(u)]
            new_w = [x + y for x, y in zip(w, b)]
            tend_ref[0, pl.ds(z, 1), :cols] = mean_b
            tend_ref[1, pl.ds(z, 1), :cols] = mean_u
            for ref, rows in ((b_ref, new_b), (u_ref, new_u), (w_ref, new_w), (p_ref, p)):
                for m, value in enumerate(side_by_side(rows)):
                    ref[z, m] = value

    for i in range(4):
        for copy in copies[4 * i : 4 * i + 4]:
            copy.wait()
        spans(cuts[i], cuts[i + 1], 4, prologue)

    def right_side(zs):
        for z in zs:
            up = jnp.minimum(z + 1, nz - 1)
            dn = jnp.maximum(z - 1, 0)
            here, cu, cd = (coef_ref[c, pl.ds(z, 1), :] for c in (3, 4, 5))
            u = [u_ref[z, m] for m in range(QUAD)]
            e, w = east_of(u, low), west_of(u, low)
            for m in range(QUAD):
                rhs_ref[z, m] = here * (e[m] - w[m]) + (cu * w_ref[up, m] + cd * w_ref[dn, m])

    spans(0, nz, 8, right_side)
    sweeps(p_ref, rhs_ref, coef_ref, low, nz)

    def middle(zs):
        done = []
        for z in zs:
            mask = jnp.broadcast_to(z < act, (8, LANES))
            fb, fu = force_ref[0, pl.ds(z, 1), :], force_ref[1, pl.ds(z, 1), :]
            p = [p_ref[z, m] for m in range(QUAD)]
            e, w = east_of(p, low), west_of(p, low)
            up, dn = jnp.minimum(z + 1, nz - 1), jnp.maximum(z - 1, 0)
            top = jnp.where(z < nz - 1, 0.5, 0.0)
            bottom = jnp.where(z > 0, 0.5, 0.0)
            us = [jnp.where(mask, u_ref[z, m] - 0.5 * (e[m] - w[m]), 0.0) for m in range(QUAD)]
            ws = [
                jnp.where(mask, w_ref[z, m] - (top * p_ref[up, m] - bottom * p_ref[dn, m]), 0.0)
                for m in range(QUAD)
            ]
            bs = [b_ref[z, m] for m in range(QUAD)]
            mean_b, mean_u, mean_w = packed_mean(bs), packed_mean(us), packed_mean(ws)
            extra = 0.25 * (fu - mean_u)
            last_b = mean_b + 0.25 * (fb - mean_b) - 0.5 * mean_w
            row = z < act
            tb = (jnp.where(row, last_b, 0.0)[:, :cols] - tend_ref[0, pl.ds(z, 1), :cols]) * (1.0 / NSTEP)
            tu = (jnp.where(row, mean_u + extra, 0.0)[:, :cols] - tend_ref[1, pl.ds(z, 1), :cols]) * (1.0 / NSTEP)
            done.append((z, tb, tu, [s + extra for s in smooth(us, low)], [x + y for x, y in zip(ws, bs)]))
        for z, tb, tu, new_u, new_w in done:
            tend_ref[0, pl.ds(z, 1), :cols] = tb
            tend_ref[1, pl.ds(z, 1), :cols] = tu
            for m in range(QUAD):
                u_ref[z, m] = new_u[m]
                b_ref[z, m] = new_w[m]

    spans(0, nz, 8, middle)
    sweeps(p_ref, rhs_ref, coef_ref, low, nz)

    def project(zs):
        for z in zs:
            mask = jnp.broadcast_to(z < act, (8, LANES))
            p = [p_ref[z, m] for m in range(QUAD)]
            e, w = east_of(p, low), west_of(p, low)
            for m in range(QUAD):
                w_ref[z, m] = jnp.where(mask, u_ref[z, m] - 0.5 * (e[m] - w[m]), 0.0)

    spans(0, nz, 8, project)
    sources = (p_ref, b_ref, w_ref)

    def step(t, carry):
        at = jnp.minimum(t, (pairs - 1) // 2)
        rows = 4 * QUAD * 8
        slots = to_slots(jnp.concatenate([s[pl.ds(4 * at, 4)].reshape(rows, LANES) for s in sources], axis=0), match_ref)
        for half in range(2):
            done = jnp.clip(2 * (t - 1) + half, 0, pairs - 1)
            for f in range(3):
                out = barrel([pltpu.roll(placed[f, done, m], shifts[m], 1) for m in range(GROUPS)], bits)
                for j in range(GROUPS):
                    stage[peer(j, me), f * pairs + done] = out[j]
        for f in range(3):
            for half in range(2):
                for m in range(GROUPS):
                    row = f * rows + 8 * (QUAD * (2 * half + m // OCT) + m % QUAD)
                    col = LANES * ((m // QUAD) % 2)
                    placed[f, 2 * at + half, m] = slots[row : row + 8, col : col + LANES]
        return carry

    stores = []
    turns = [0, 6, 11, (pairs + 1) // 2 + 1]
    for i in range(3):
        lax.fori_loop(turns[i], turns[i + 1], step, 0)
        start, stop = max(2 * (turns[i] - 1), 0), min(2 * (turns[i + 1] - 1), pairs)
        for f in range(3):
            part = pl.ds(f * pairs + start, stop - start)
            copy = pltpu.make_async_copy(stage.at[:, part], send.at[:, part], out_sems.at[i, f])
            copy.start()
            stores.append(copy)
    for copy in stores:
        copy.wait()


def last_kernel(
    got_b, got, dyn_ref, prev_y, next_y, tend_ref, orient_ref,
    out, dyn_out,
    rolled, pressure, stage, out_sems,
):
    nz = stage.shape[1]
    pairs = nz // 2
    cols, levels = dyn_ref.shape[1:]
    me = lax.axis_index("gx")
    bits = group_bits()
    group = lane_ids() // RANKS
    act = jnp.zeros((8, LANES), jnp.float32)
    for source in range(GROUPS):
        ranks = pltpu.roll(got_b[source, pairs + 1], (RANKS * source + LANES - TAIL) % LANES, 1)
        act = jnp.where(group == source, ranks, act)
    full = act > 0.0
    for m in range(OCT):
        pressure[0, m] = jnp.zeros((8, LANES), jnp.float32)
        pressure[nz + 1, m] = jnp.zeros((8, LANES), jnp.float32)
    shifts = [lax.rem(2 * GROUPS - m - me, GROUPS) * RANKS for m in range(GROUPS)]
    peers = [peer(j, me) for j in range(GROUPS)]

    def place(g, m16):
        z, m = 2 * g + m16 // OCT, m16 % OCT
        mask = z.astype(jnp.float32) < act
        row = pl.ds(m, 8, stride=8)
        w = rolled[0, g, m16]
        gradient = pressure[z + 2, m] - pressure[z, m]
        stage[0, z, row, :] = jnp.where(full, rolled[1, g, m16], 0.0)
        stage[1, z, row, :] = jnp.where(mask, w - 0.5 * gradient, 0.0)
        stage[2, z, row, :] = jnp.where(mask, rolled[2, g, m16] - 0.5 * w, 0.0)
        stage[3, z, row, :] = pressure[z + 1, m]

    def keep(f, g, rows):
        for m16 in range(GROUPS):
            if f == 0:
                pressure[2 * g + m16 // OCT + 1, m16 % OCT] = jnp.where(full, rows[m16], 0.0)
            else:
                rolled[f - 1, g, m16] = rows[m16]

    def step(t, carry):
        last = None
        for half in range(2):
            done = jnp.clip(2 * t + half - 3, 0, pairs - 1)
            g = jnp.minimum(2 * t + half, pairs - 1)
            for f, (ref, at) in enumerate(((got, g), (got, pairs + g), (got, 2 * pairs + g), (got_b, g))):
                rows = barrel([ref[peers[j], at] for j in range(GROUPS)], bits)
                rows = [pltpu.roll(rows[m16], shifts[m16], 1) for m16 in range(GROUPS)]
                if last is not None:
                    keep(*last)
                for m16 in range(4 * f, 4 * f + 4):
                    place(done, m16)
                last = (f, g, rows)
        keep(*last)
        return carry

    stores = []
    turns = [0, 5, 8, 11, 14, (pairs + 4) // 2]
    for i in range(5):
        lax.fori_loop(turns[i], turns[i + 1], step, 0)
        start, stop = max(2 * turns[i] - 3, 0), min(2 * turns[i + 1] - 3, pairs)
        part = pl.ds(2 * start, 2 * (stop - start))
        for f in range(4):
            copy = pltpu.make_async_copy(stage.at[f, part], out.at[f, part], out_sems.at[i, f])
            copy.start()
            stores.append(copy)

    left, right = lax.rem(me + GROUPS - 1, GROUPS), lax.rem(me + 1, GROUPS)
    col = lax.broadcasted_iota(jnp.int32, (cols, levels), 0)
    first_b, last_b = col % 8 == 0, col % 8 == 7
    first = jnp.broadcast_to(to_column(orient_ref[...].astype(jnp.float32), cols), (cols, levels)) < 0.5
    adds = [jnp.transpose(tend_ref[i])[:cols, :levels] for i in range(2)]
    adds = [adds[0], jnp.where(first, adds[1], 0.0), jnp.where(first, 0.0, adds[1])]

    def turned(value, by):
        by = by % cols
        return jnp.concatenate([value[cols - by :], value[: cols - by]], axis=0)

    lane = lane_ids()
    before, after = (
        edge_fields(got_b[at, pairs], got_b[at, pairs + 1], lane, levels) for at in (left, right)
    )
    for f in range(3):
        here = dyn_ref[f]
        up_x = jnp.concatenate([before[f][:, :levels], here[: cols - 8]], axis=0)
        dn_x = jnp.concatenate([here[8:], after[f][:, :levels]], axis=0)
        up_y = jnp.where(first_b, turned(prev_y[f], -7), turned(here, 1))
        dn_y = jnp.where(last_b, turned(next_y[f], 7), turned(here, -1))
        dyn_out[f] = (here + 0.2 * ((up_x + dn_x) + (up_y + dn_y) - 4.0 * here)) + adds[f]
    for copy in stores:
        copy.wait()


def per_device(dynamics, crm_state, density, orientation, owner, active):
    nz, nx, cols = crm_state.shape[1:]
    levels = dynamics.shape[1]
    pairs = nz // 2
    f32 = jnp.float32
    vmem = pl.BlockSpec(memory_space=pltpu.VMEM)
    hbm = pl.BlockSpec(memory_space=pltpu.HBM)
    shape = jax.ShapeDtypeStruct
    dma = pltpu.SemaphoreType.DMA
    square = pltpu.VMEM((LANES, LANES), f32)
    turned = jnp.swapaxes(dynamics, 1, 2)
    owner_row, active_row, orient_row = owner[None], active[None], orientation[None]
    density_row = density[None]
    state_in = pltpu.with_memory_space_constraint(crm_state, pltpu.HBM)

    def params(mib):
        return pltpu.CompilerParams(vmem_limit_bytes=mib * MIB)

    def neighbour(field, axis, by):
        count = lax.axis_size(axis)
        return lax.ppermute(field, axis, [(i, (i + by) % count) for i in range(count)])

    send_b = pl.pallas_call(
        early_kernel,
        out_shape=pltpu.HBM((GROUPS, pairs + 2, 8, LANES), f32),
        in_specs=[hbm] * 4,
        out_specs=hbm,
        scratch_shapes=[
            pltpu.VMEM((nz, nx, cols), f32),
            pltpu.VMEM((nz, nx, cols), f32),
            pltpu.VMEM((3, cols, levels), f32),
            pltpu.VMEM((3, cols, LANES), f32),
            pltpu.VMEM((1, cols), jnp.int32),
            pltpu.VMEM((1, cols), jnp.int32),
            square,
            square,
            pltpu.VMEM((nz + 2, OCT, 8, LANES), f32),
            pltpu.VMEM((pairs + 1, GROUPS, 8, LANES), f32),
            pltpu.VMEM((GROUPS, pairs + 2, 8, LANES), f32),
            pltpu.VMEM((GROUPS, 8, LANES), jnp.int32),
            dma((5, 2)),
            dma((3,)),
            dma((5,)),
        ],
        compiler_params=params(16),
        name="early_buoyancy",
    )(state_in, *(pltpu.with_memory_space_constraint(x, pltpu.HBM) for x in (turned, owner_row, active_row)))
    got_b = lax.all_to_all(send_b, "gx", 0, 0, tiled=True)

    state = pltpu.VMEM((nz + 2, QUAD, 8, LANES), f32)
    send, tends = pl.pallas_call(
        main_kernel,
        out_shape=[pltpu.HBM((GROUPS, 3 * pairs, 8, LANES), f32), shape((2, LANES, LANES), f32)],
        in_specs=[hbm, vmem, vmem, vmem, vmem, vmem],
        out_specs=[hbm, vmem],
        scratch_shapes=[pltpu.VMEM((4, nz, nx, cols), f32)]
        + [state] * 5
        + [
            pltpu.VMEM((6, HALF, LANES), f32),
            pltpu.VMEM((3 * LANES, 2 * LANES), jnp.bfloat16),
            square,
            pltpu.VMEM((2, LANES, LANES), f32),
            pltpu.VMEM((3, pairs + 1, GROUPS, 8, LANES), f32),
            pltpu.VMEM((GROUPS, 3 * pairs, 8, LANES), f32),
            dma((4, 4)),
            dma((3, 3)),
        ],
        compiler_params=params(28),
        cost_estimate=pl.CostEstimate(flops=60_000_000, bytes_accessed=14_000_000, transcendentals=0),
        name="cloud_steps",
    )(state_in, turned, orient_row, owner_row, active_row, density_row)
    prev_y, next_y = neighbour(turned, "gy", 1), neighbour(turned, "gy", -1)
    got_b, send, tends, prev_y, next_y = lax.optimization_barrier((got_b, send, tends, prev_y, next_y))
    got = lax.all_to_all(send, "gx", 0, 0, tiled=True)

    crm_next, dynamics_next = pl.pallas_call(
        last_kernel,
        out_shape=[pltpu.HBM((4, nz, nx, LANES), f32), shape(turned.shape, f32)],
        in_specs=[vmem] * 7,
        out_specs=[hbm, vmem],
        scratch_shapes=[
            pltpu.VMEM((3, pairs, GROUPS, 8, LANES), f32),
            pltpu.VMEM((nz + 2, OCT, 8, LANES), f32),
            pltpu.VMEM((4, nz, nx, LANES), f32),
            dma((5, 4)),
        ],
        compiler_params=params(20),
        name="place_state",
    )(got_b, got, turned, prev_y, next_y, tends, orient_row)
    return (jnp.swapaxes(dynamics_next, 1, 2), crm_next)


def solution(mesh):
    in_specs = (
        P(None, None, ("gx", "gy")),
        P(None, None, None, ("gx", "gy")),
        P(),
        P(("gx", "gy")),
        P(("gx", "gy")),
        P(("gx", "gy")),
    )
    out_specs = (P(None, None, ("gx", "gy")), P(None, None, None, ("gx", "gy")))
    return jax.shard_map(
        per_device, mesh=mesh, in_specs=in_specs, out_specs=out_specs, check_vma=False
    )
```

time: 132 us -> 118 us (0.89)
  Pallas kernels: 44.8 us -> 29.9 us
  waiting for transfers between devices: 0.01 us -> 8.27 us
  blocking collectives: 73.2 us -> 68.5 us
  local copies, waits for them, and re-layouts: 2.52 us -> 0.02 us
    pallas_call x4 -> x3, Pallas kernels: 44.8 us -> 29.9 us  [the longest x1 18 us: per_device(): pl.pallas_call(main_kernel, out_shape=[pltpu.HBM((GROUPS, 3 * pairs, 8, L...]
    all_to_all x1, waiting for transfers between devices: 0.01 us -> 8.26 us  [per_device(): got_b = lax.all_to_all(send_b, 'gx', 0, 0, tiled=True)]
    all_to_all x1, blocking collectives: 73.2 us -> 68.5 us  [per_device(): got = lax.all_to_all(send, 'gx', 0, 0, tiled=True)]
    unnamed x12 -> x10, local copies, waits for them, and re-layouts: 2.52 us -> 0.02 us
  transfers between devices with their start and end apart: 3 -> 3, of which waited for: 0 -> 1; matrix products, arithmetic and copies ran while one was open for 0% -> 0% of each run, Pallas kernels for 21% -> 15%
where the time goes in v2:
time: 118 us
  blocking collectives  68.5 us (58%)
  Pallas kernels  29.9 us (25%)
  starting transfers between devices  10.3 us (9%)
  waiting for transfers between devices  8.27 us (7%)
    all_to_all x1, blocking collectives, per_device(): got = lax.all_to_all(send, 'gx', 0, 0, tiled=True)  68.5 us
    pallas_call x1, Pallas kernels, per_device(): pl.pallas_call(main_kernel, out_shape=[pltpu.HBM((GROUPS, 3 * pairs, 8, L...  18 us
    all_to_all x1, waiting for transfers between devices, per_device(): got_b = lax.all_to_all(send_b, 'gx', 0, 0, tiled=True)  8.26 us
    all_to_all x1, starting transfers between devices, per_device(): got_b = lax.all_to_all(send_b, 'gx', 0, 0, tiled=True)  7.13 us
    pallas_call x1, Pallas kernels, per_device(): pl.pallas_call(early_kernel, out_shape=pltpu.HBM((GROUPS, pairs + 2, 8, L...  6.11 us
    pallas_call x1, Pallas kernels, per_device(): pl.pallas_call(last_kernel, out_shape=[pltpu.HBM((4, nz, nx, LANES), f32)...  5.76 us
    ppermute x2, starting transfers between devices, neighbour(): lax.ppermute(field, axis, [(i, (i + by) % count) for i in range(count)])  3.21 us
  transfers between devices with their start and end apart: 3, of which 1 were waited for; matrix products, arithmetic and copies ran while one was open for 0% of the time, Pallas kernels for 15%

profile of v2, /device:TPU:0, one launch (start us, length us, event | category | flops | bytes accessed | tf_op | source)
XLA Modules:
  0.0 117.8 jit_solution(6733859979273886184)
XLA Ops:
  0.6 0.0 copy-start
  0.6 0.0 copy-start.1
  0.7 0.0 copy-start.2
  0.7 0.0 copy-start.3
  0.7 0.0 copy-start.4
  0.7 6.1 %early_buoyancy.1 = f32[16,31,8,128]{3,2,1,0:T(8,128)} custom-call(f32[4,58,64,64]{3,2,1,0:T(8,128)} %crm.3, f32[3,64,72]{2,1,0:T(8,128)} %bitcast.6, s32[1,64]{1,0:T(1,128)} %bitcast.11, s32[1,64]{1,0:T(1,128)} %bitcast.13), custom_call_target="tpu_custom_call" | custom-call | tf_op jit(solution)/shard_map/early_buoyancy/pallas_call | solution.py:562
  6.8 7.1 %all-to-all-start = ((f32[16,31,8,128]{3,2,1,0:T(8,128)}), f32[16,31,8,128]{3,2,1,0:T(8,128)S(1)}, u32[]{:S(2)}, u32[]{:S(2)}) async-start(f32[16,31,8,128]{3,2,1,0:T(8,128)} %early_buoyancy.1), calls=%async_computation | async-start | bytes 4063232 | tf_op jit(solution)/shard_map/all_to_all | solution.py:587
  13.9 0.0 copy-done
  13.9 3.2 %collective-permute-start.1 = (f32[3,64,72]{2,1,0:T(8,128)S(1)}, f32[3,64,72]{2,1,0:T(8,128)S(1)}, u32[]{:S(2)}, u32[]{:S(2)}) collective-permute-start(f32[3,64,72]{2,1,0:T(8,128)S(1)} %bitcast.7), channel_id=1, source_target_pairs={{0,7},{1,0},{2,1},{3,2},{4,3},{5,4},{6,5},{7,6},{8,15},{9,8},{10,9... | collective-permute-start | bytes 165896 | tf_op jit(solution)/shard_map/ppermute | solution.py:560
  17.2 0.0 collective-permute-start
  17.2 0.0 copy-done.1
  17.2 0.0 copy-done.2
  17.2 0.0 copy-done.3
  17.2 0.0 copy-done.4
  17.2 18.0 %cloud_steps.1 = (f32[16,87,8,128]{3,2,1,0:T(8,128)}, f32[2,128,128]{2,1,0:T(8,128)S(1)}) custom-call(f32[4,58,64,64]{3,2,1,0:T(8,128)} %crm.3, f32[3,64,72]{2,1,0:T(8,128)S(1)} %bitcast.9, s32[1,64]{1,0:T(1,128)S(1)} %bitcast.15, s32[1,64]{1,0:T(1,128)S(1)} %bitcast.12, s32[1,64]{1,0:T(1,128)S(1)} %bitcast.14, f32[1,58]{1,0:T(1,128)S(1)} %bitcast.17), custom_call_target="tpu_custom_call" | custom-call | flops 60000000 | bytes 14000000 | tf_op jit(solution)/shard_map/cloud_steps/pallas_call | solution.py:590
  35.2 0.0 collective-permute-done.1.next_y
  35.2 0.0 collective-permute-done.prev_y
  35.2 8.3 %all-to-all-done.got_b = f32[16,31,8,128]{3,2,1,0:T(8,128)S(1)} async-done(((f32[16,31,8,128]{3,2,1,0:T(8,128)}), f32[16,31,8,128]{3,2,1,0:T(8,128)S(1)}, u32[]{:S(2)}, u32[]{:S(2)}) %all-to-all-start) | async-done | bytes 2031648 | tf_op jit(solution)/shard_map/all_to_all | solution.py:587
  43.5 68.5 %all_to_all.10.got = f32[16,87,8,128]{3,2,1,0:T(8,128)S(1)} all-to-all(f32[16,87,8,128]{3,2,1,0:T(8,128)} %get-tuple-element.14), channel_id=1, replica_groups=mesh['gx'=16,'gy'=8] {'gx'}, dimensions={0} | all-to-all | bytes 11403264 | tf_op jit(solution)/shard_map/all_to_all | solution.py:613
  112.0 5.8 %place_state.1 = (f32[4,58,64,128]{3,2,1,0:T(8,128)}, f32[3,64,72]{2,1,0:T(8,128)}) custom-call(f32[16,31,8,128]{3,2,1,0:T(8,128)S(1)} %all-to-all-done.got_b, f32[16,87,8,128]{3,2,1,0:T(8,128)S(1)} %all_to_all.10.got, f32[3,64,72]{2,1,0:T(8,128)S(1)} %bitcast.10, f32[3,64,72]{2,1,0:T(8,128)S(1)} %collective-permute-done.prev_y, ...), custom_call_target="tpu_custom_call" | custom-call | tf_op jit(solution)/shard_map/place_state/pallas_call | solution.py:615
Async XLA Ops:
  0.6 13.3 %copy-start = (f32[3,72,64]{1,2,0:T(8,128)S(1)}, f32[3,72,64]{1,2,0:T(8,128)}, u32[]{:S(2)}) copy-start(f32[3,72,64]{1,2,0:T(8,128)} %param.6) | copy-start | bytes 165892
  0.6 16.5 %copy-start.1 = (s32[64]{0:T(128)S(1)}, s32[64]{0:T(128)}, u32[]{:S(2)}) copy-start(s32[64]{0:T(128)} %param.10) | copy-start | bytes 772
  0.7 16.5 %copy-start.2 = (s32[64]{0:T(128)S(1)}, s32[64]{0:T(128)}, u32[]{:S(2)}) copy-start(s32[64]{0:T(128)} %param.11) | copy-start | bytes 772
  0.7 16.5 %copy-start.3 = (s32[64]{0:T(128)S(1)}, s32[64]{0:T(128)}, u32[]{:S(2)}) copy-start(s32[64]{0:T(128)} %param.9) | copy-start | bytes 772
  0.7 16.5 %copy-start.4 = (f32[58]{0:T(128)S(1)}, f32[58]{0:T(128)}, u32[]{:S(2)}) copy-start(f32[58]{0:T(128)} %param.8) | copy-start | bytes 700
  6.8 36.7 %all-to-all-start = ((f32[16,31,8,128]{3,2,1,0:T(8,128)}), f32[16,31,8,128]{3,2,1,0:T(8,128)S(1)}, u32[]{:S(2)}, u32[]{:S(2)}) async-start(f32[16,31,8,128]{3,2,1,0:T(8,128)} %early_buoyancy.1), calls=%async_computation | async-start | bytes 4063232 | tf_op jit(solution)/shard_map/all_to_all | solution.py:587
  13.9 21.3 %collective-permute-start.1 = (f32[3,64,72]{2,1,0:T(8,128)S(1)}, f32[3,64,72]{2,1,0:T(8,128)S(1)}, u32[]{:S(2)}, u32[]{:S(2)}) collective-permute-start(f32[3,64,72]{2,1,0:T(8,128)S(1)} %bitcast.7), channel_id=1, source_target_pairs={{0,7},{1,0},{2,1},{3,2},{4,3},{5,4},{6,5},{7,6},{8,15},{9,8},{10,9... | collective-permute-start | bytes 165896 | tf_op jit(solution)/shard_map/ppermute | solution.py:560
  17.2 18.1 %collective-permute-start = (f32[3,64,72]{2,1,0:T(8,128)S(1)}, f32[3,64,72]{2,1,0:T(8,128)S(1)}, u32[]{:S(2)}, u32[]{:S(2)}) collective-permute-start(f32[3,64,72]{2,1,0:T(8,128)S(1)} %bitcast.8), channel_id=1, source_target_pairs={{0,1},{1,2},{2,3},{3,4},{4,5},{5,6},{6,7},{7,0},{8,9},{9,10},{10,1... | collective-permute-start | bytes 165896 | tf_op jit(solution)/shard_map/ppermute | solution.py:560

commit v3 on v2

--- a/solution.py
+++ b/solution.py
@@ -472,17 +472,21 @@
         row = pl.ds(m, 8, stride=8)
         w = rolled[0, g, m16]
         gradient = pressure[z + 2, m] - pressure[z, m]
-        stage[0, z, row, :] = jnp.where(full, rolled[1, g, m16], 0.0)
         stage[1, z, row, :] = jnp.where(mask, w - 0.5 * gradient, 0.0)
-        stage[2, z, row, :] = jnp.where(mask, rolled[2, g, m16] - 0.5 * w, 0.0)
-        stage[3, z, row, :] = pressure[z + 1, m]
+        stage[2, z, row, :] = jnp.where(mask, rolled[1, g, m16] - 0.5 * w, 0.0)
 
     def keep(f, g, rows):
         for m16 in range(GROUPS):
+            z, m = 2 * g + m16 // OCT, m16 % OCT
+            row = pl.ds(m, 8, stride=8)
             if f == 0:
-                pressure[2 * g + m16 // OCT + 1, m16 % OCT] = jnp.where(full, rows[m16], 0.0)
+                value = jnp.where(full, rows[m16], 0.0)
+                pressure[z + 1, m] = value
+                stage[3, z, row, :] = value
+            elif f == 2:
+                stage[0, z, row, :] = jnp.where(full, rows[m16], 0.0)
             else:
-                rolled[f - 1, g, m16] = rows[m16]
+                rolled[f // 2, g, m16] = rows[m16]
 
     def step(t, carry):
         last = None
@@ -618,7 +622,7 @@
         in_specs=[vmem] * 7,
         out_specs=[hbm, vmem],
         scratch_shapes=[
-            pltpu.VMEM((3, pairs, GROUPS, 8, LANES), f32),
+            pltpu.VMEM((2, pairs, GROUPS, 8, LANES), f32),
             pltpu.VMEM((nz + 2, OCT, 8, LANES), f32),
             pltpu.VMEM((4, nz, nx, LANES), f32),
             dma((5, 4)),

time: 118 us -> 118 us (level)
  no operation moved by 1% of the time
where the time goes in v3:
time: 118 us
  blocking collectives  68.5 us (58%)
  Pallas kernels  29.8 us (25%)
  starting transfers between devices  10.3 us (9%)
  waiting for transfers between devices  8.27 us (7%)
    all_to_all x1, blocking collectives, per_device(): got = lax.all_to_all(send, 'gx', 0, 0, tiled=True)  68.5 us
    pallas_call x1, Pallas kernels, per_device(): pl.pallas_call(main_kernel, out_shape=[pltpu.HBM((GROUPS, 3 * pairs, 8, L...  18 us
    all_to_all x1, waiting for transfers between devices, per_device(): got_b = lax.all_to_all(send_b, 'gx', 0, 0, tiled=True)  8.26 us
    all_to_all x1, starting transfers between devices, per_device(): got_b = lax.all_to_all(send_b, 'gx', 0, 0, tiled=True)  7.13 us
    pallas_call x1, Pallas kernels, per_device(): pl.pallas_call(early_kernel, out_shape=pltpu.HBM((GROUPS, pairs + 2, 8, L...  6.11 us
    pallas_call x1, Pallas kernels, per_device(): pl.pallas_call(last_kernel, out_shape=[pltpu.HBM((4, nz, nx, LANES), f32)...  5.73 us
    ppermute x2, starting transfers between devices, neighbour(): lax.ppermute(field, axis, [(i, (i + by) % count) for i in range(count)])  3.21 us
  transfers between devices with their start and end apart: 3, of which 1 were waited for; matrix products, arithmetic and copies ran while one was open for 0% of the time, Pallas kernels for 15%

profile of v3, /device:TPU:0, one launch (start us, length us, event | category | flops | bytes accessed | tf_op | source)
XLA Modules:
  0.0 117.7 jit_solution(111853149470354705)
XLA Ops:
  0.6 0.0 copy-start
  0.6 0.0 copy-start.1
  0.7 0.0 copy-start.2
  0.7 0.0 copy-start.3
  0.7 0.0 copy-start.4
  0.7 6.1 %early_buoyancy.1 = f32[16,31,8,128]{3,2,1,0:T(8,128)} custom-call(f32[4,58,64,64]{3,2,1,0:T(8,128)} %crm.3, f32[3,64,72]{2,1,0:T(8,128)} %bitcast.6, s32[1,64]{1,0:T(1,128)} %bitcast.11, s32[1,64]{1,0:T(1,128)} %bitcast.13), custom_call_target="tpu_custom_call" | custom-call | tf_op jit(solution)/shard_map/early_buoyancy/pallas_call | solution.py:566
  6.8 7.1 %all-to-all-start = ((f32[16,31,8,128]{3,2,1,0:T(8,128)}), f32[16,31,8,128]{3,2,1,0:T(8,128)S(1)}, u32[]{:S(2)}, u32[]{:S(2)}) async-start(f32[16,31,8,128]{3,2,1,0:T(8,128)} %early_buoyancy.1), calls=%async_computation | async-start | bytes 4063232 | tf_op jit(solution)/shard_map/all_to_all | solution.py:591
  13.9 0.0 copy-done
  13.9 3.2 %collective-permute-start.1 = (f32[3,64,72]{2,1,0:T(8,128)S(1)}, f32[3,64,72]{2,1,0:T(8,128)S(1)}, u32[]{:S(2)}, u32[]{:S(2)}) collective-permute-start(f32[3,64,72]{2,1,0:T(8,128)S(1)} %bitcast.7), channel_id=1, source_target_pairs={{0,7},{1,0},{2,1},{3,2},{4,3},{5,4},{6,5},{7,6},{8,15},{9,8},{10,9... | collective-permute-start | bytes 165896 | tf_op jit(solution)/shard_map/ppermute | solution.py:564
  17.2 0.0 collective-permute-start
  17.2 0.0 copy-done.1
  17.2 0.0 copy-done.2
  17.2 0.0 copy-done.3
  17.2 0.0 copy-done.4
  17.2 18.0 %cloud_steps.1 = (f32[16,87,8,128]{3,2,1,0:T(8,128)}, f32[2,128,128]{2,1,0:T(8,128)S(1)}) custom-call(f32[4,58,64,64]{3,2,1,0:T(8,128)} %crm.3, f32[3,64,72]{2,1,0:T(8,128)S(1)} %bitcast.9, s32[1,64]{1,0:T(1,128)S(1)} %bitcast.15, s32[1,64]{1,0:T(1,128)S(1)} %bitcast.12, s32[1,64]{1,0:T(1,128)S(1)} %bitcast.14, f32[1,58]{1,0:T(1,128)S(1)} %bitcast.17), custom_call_target="tpu_custom_call" | custom-call | flops 60000000 | bytes 14000000 | tf_op jit(solution)/shard_map/cloud_steps/pallas_call | solution.py:594
  35.2 0.0 collective-permute-done.1.next_y
  35.2 0.0 collective-permute-done.prev_y
  35.2 8.3 %all-to-all-done.got_b = f32[16,31,8,128]{3,2,1,0:T(8,128)S(1)} async-done(((f32[16,31,8,128]{3,2,1,0:T(8,128)}), f32[16,31,8,128]{3,2,1,0:T(8,128)S(1)}, u32[]{:S(2)}, u32[]{:S(2)}) %all-to-all-start) | async-done | bytes 2031648 | tf_op jit(solution)/shard_map/all_to_all | solution.py:591
  43.5 68.5 %all_to_all.10.got = f32[16,87,8,128]{3,2,1,0:T(8,128)S(1)} all-to-all(f32[16,87,8,128]{3,2,1,0:T(8,128)} %get-tuple-element.14), channel_id=1, replica_groups=mesh['gx'=16,'gy'=8] {'gx'}, dimensions={0} | all-to-all | bytes 11403264 | tf_op jit(solution)/shard_map/all_to_all | solution.py:617
  112.0 5.7 %place_state.1 = (f32[4,58,64,128]{3,2,1,0:T(8,128)}, f32[3,64,72]{2,1,0:T(8,128)}) custom-call(f32[16,31,8,128]{3,2,1,0:T(8,128)S(1)} %all-to-all-done.got_b, f32[16,87,8,128]{3,2,1,0:T(8,128)S(1)} %all_to_all.10.got, f32[3,64,72]{2,1,0:T(8,128)S(1)} %bitcast.10, f32[3,64,72]{2,1,0:T(8,128)S(1)} %collective-permute-done.prev_y, ...), custom_call_target="tpu_custom_call" | custom-call | tf_op jit(solution)/shard_map/place_state/pallas_call | solution.py:619
Async XLA Ops:
  0.6 13.3 %copy-start = (f32[3,72,64]{1,2,0:T(8,128)S(1)}, f32[3,72,64]{1,2,0:T(8,128)}, u32[]{:S(2)}) copy-start(f32[3,72,64]{1,2,0:T(8,128)} %param.6) | copy-start | bytes 165892
  0.6 16.5 %copy-start.1 = (s32[64]{0:T(128)S(1)}, s32[64]{0:T(128)}, u32[]{:S(2)}) copy-start(s32[64]{0:T(128)} %param.10) | copy-start | bytes 772
  0.7 16.5 %copy-start.2 = (s32[64]{0:T(128)S(1)}, s32[64]{0:T(128)}, u32[]{:S(2)}) copy-start(s32[64]{0:T(128)} %param.11) | copy-start | bytes 772
  0.7 16.5 %copy-start.3 = (s32[64]{0:T(128)S(1)}, s32[64]{0:T(128)}, u32[]{:S(2)}) copy-start(s32[64]{0:T(128)} %param.9) | copy-start | bytes 772
  0.7 16.5 %copy-start.4 = (f32[58]{0:T(128)S(1)}, f32[58]{0:T(128)}, u32[]{:S(2)}) copy-start(f32[58]{0:T(128)} %param.8) | copy-start | bytes 700
  6.8 36.7 %all-to-all-start = ((f32[16,31,8,128]{3,2,1,0:T(8,128)}), f32[16,31,8,128]{3,2,1,0:T(8,128)S(1)}, u32[]{:S(2)}, u32[]{:S(2)}) async-start(f32[16,31,8,128]{3,2,1,0:T(8,128)} %early_buoyancy.1), calls=%async_computation | async-start | bytes 4063232 | tf_op jit(solution)/shard_map/all_to_all | solution.py:591
  13.9 21.3 %collective-permute-start.1 = (f32[3,64,72]{2,1,0:T(8,128)S(1)}, f32[3,64,72]{2,1,0:T(8,128)S(1)}, u32[]{:S(2)}, u32[]{:S(2)}) collective-permute-start(f32[3,64,72]{2,1,0:T(8,128)S(1)} %bitcast.7), channel_id=1, source_target_pairs={{0,7},{1,0},{2,1},{3,2},{4,3},{5,4},{6,5},{7,6},{8,15},{9,8},{10,9... | collective-permute-start | bytes 165896 | tf_op jit(solution)/shard_map/ppermute | solution.py:564
  17.2 18.1 %collective-permute-start = (f32[3,64,72]{2,1,0:T(8,128)S(1)}, f32[3,64,72]{2,1,0:T(8,128)S(1)}, u32[]{:S(2)}, u32[]{:S(2)}) collective-permute-start(f32[3,64,72]{2,1,0:T(8,128)S(1)} %bitcast.8), channel_id=1, source_target_pairs={{0,1},{1,2},{2,3},{3,4},{4,5},{5,6},{6,7},{7,0},{8,9},{9,10},{10,1... | collective-permute-start | bytes 165896 | tf_op jit(solution)/shard_map/ppermute | solution.py:564
